TPU v7x, 32 devices: a whole 2x2x4 slice. The times are simulated.
32 devices in a mesh: dp: 16 (over z, y, core), mp: 2 (over x).
Axes of the slice: x: 2, y: 2, z: 4, core: 2. Of those that a mesh axis runs over, the one named last changes fastest.
Arguments:
- tokens: bfloat16 [32768, 1024], P(('dp', 'mp')), may hold values from -6 to 6
- cotangent: bfloat16 [32768, 1024], P(('dp', 'mp')), may hold values from -18 to 18
- lengths: int32 [16, 8], P('dp'), may hold values from 1 to 1280, 2048 in all within a row
- pad_count: int32 [16], P('dp'), may hold values from 0 to 256
- ln1_gain: float32 [1024], replicated, may hold values from 0.5 to 1.5
- ln1_bias: float32 [1024], replicated, may hold values from -4 to 4
- ln2_gain: float32 [1024], replicated, may hold values from 0.5 to 1.5
- ln2_bias: float32 [1024], replicated, may hold values from -4 to 4
- qkv_weight: bfloat16 [1024, 3, 1024], P(None, None, 'mp'), may hold values from -0.1875 to 0.1875
- qkv_bias: float32 [3, 1024], P(None, 'mp'), may hold values from -6 to 6
- out_weight: bfloat16 [1024, 1024], P('mp'), may hold values from -1 to 1
- out_bias: float32 [1024], replicated, may hold values from -6 to 6
- fc1_weight: bfloat16 [1024, 4096], P(None, 'mp'), may hold values from -0.1875 to 0.1875
- fc1_bias: float32 [4096], P('mp'), may hold values from -6 to 6
- fc2_weight: bfloat16 [4096, 1024], P('mp'), may hold values from -0.09375 to 0.09375
Outputs:
- output: bfloat16 [32768, 1024], P(('dp', 'mp'))
- grad_tokens: float32 [32768, 1024], P(('dp', 'mp'))
- grad_ln1_gain: float32 [1024], replicated
- grad_ln1_bias: float32 [1024], replicated
- grad_ln2_gain: float32 [1024], replicated
- grad_ln2_bias: float32 [1024], replicated
- grad_qkv_weight: float32 [1024, 3, 1024], P(None, None, 'mp')
- grad_qkv_bias: float32 [3, 1024], P(None, 'mp')
- grad_out_weight: float32 [1024, 1024], P('mp')
- grad_out_bias: float32 [1024], replicated
- grad_fc1_weight: float32 [1024, 4096], P(None, 'mp')
- grad_fc1_bias: float32 [4096], P('mp')
- grad_fc2_weight: float32 [4096, 1024], P('mp')
Inputs may be any that keep to these rules, and one draw needn't show every extreme that they name: Each row lists its 8 document lengths in order; they sum to 2048 and the largest is exactly 1280.
All inputs are finite; a program needn't handle non-finite values.
Results may differ from a plain program's by a relative error of at most 0.012.
Values may be sent and summed in bfloat16 or wider, within the bound.
No kernel may reach another device: no remote copies, remote signals or barrier semaphores. Data moves between devices by JAX's collectives and lax.ppermute only.
A program may use at most 448 MiB of HBM per device.

v0:
```python
from functools import partial

import jax
import jax.numpy as jnp
from jax import lax
from jax.sharding import PartitionSpec as P

HEAD = 64
ROT = 16


EPSILON = 1e-05
MASKED_SCORE = -1e30
ROTARY_BASE = 10000.0


def layer_norm(v, gain, shift):
    average = jnp.mean(v, axis=-1, keepdims=True)
    centred = v - average
    spread = jnp.mean(centred * centred, axis=-1, keepdims=True)
    return centred * lax.rsqrt(spread + EPSILON) * gain + shift


def exact_gelu(v):
    return jax.nn.gelu(v, approximate=False)


def row_layout(row_lengths, pad_tokens, row_len):
    doc_ends = jnp.cumsum(row_lengths)
    doc_starts = doc_ends - row_lengths
    places = jnp.arange(row_len, dtype=jnp.int32)
    segment = jnp.sum((places[:, None] >= doc_ends[None, :]).astype(jnp.int32), axis=1)
    owners = segment[:, None] == jnp.arange(row_lengths.shape[0], dtype=jnp.int32)[None, :]
    doc_start = jnp.sum(jnp.where(owners, doc_starts[None, :], 0), axis=1)
    position = places - doc_start
    keep_mask = places < row_len - pad_tokens
    return (segment, position, keep_mask)


def rotary(v, position):
    half_rot = ROT // 2
    frequency = ROTARY_BASE ** (-(jnp.arange(half_rot, dtype=jnp.float32) * 2.0) / ROT)
    angles = position.astype(jnp.float32)[:, None] * frequency[None, :]
    cosine = jnp.concatenate([jnp.cos(angles), jnp.cos(angles)], axis=1)[:, None, :]
    sine_table = jnp.concatenate([jnp.sin(angles), jnp.sin(angles)], axis=1)[:, None, :]
    turned = v[..., :ROT]
    front_half = turned[..., :half_rot]
    back_half = turned[..., half_rot:]
    rolled = jnp.concatenate([-back_half, front_half], axis=-1)
    return jnp.concatenate([turned * cosine + rolled * sine_table, v[..., ROT:]], axis=-1)


def allowed_pairs(seg_rows, keep_rows, place_rows, seg_cols, keep_cols, place_cols):
    joined = (seg_rows[:, None] == seg_cols[None, :]) & keep_rows[:, None] & keep_cols[None, :]
    joined = joined & (place_cols[None, :] <= place_rows[:, None])
    return joined | (place_cols[None, :] == place_rows[:, None])


def block_scores(queries, key_rot, segment, keep_mask, block_start, block_end):
    places = jnp.arange(block_end, dtype=jnp.int32)
    scores = jnp.einsum(
        "qhd,khd->hqk",
        queries[block_start:block_end],
        key_rot[:block_end],
        preferred_element_type=jnp.float32,
    ) * HEAD ** (-0.5)
    legal = allowed_pairs(
        segment[block_start:block_end],
        keep_mask[block_start:block_end],
        places[block_start:block_end],
        segment[:block_end],
        keep_mask[:block_end],
        places,
    )
    return jnp.where(legal[None], scores, MASKED_SCORE)


def attend_forward(queries, key_rot, values, segment, keep_mask, block_rows):
    row_len = queries.shape[0]
    pieces, log_totals = ([], [])
    for block_start in range(0, row_len, block_rows):
        block_end = block_start + block_rows
        masked = block_scores(queries, key_rot, segment, keep_mask, block_start, block_end)
        largest = jnp.max(masked, axis=-1, keepdims=True)
        expo = jnp.exp(masked - largest)
        denominator = jnp.sum(expo, axis=-1, keepdims=True)
        probs_low = (expo / denominator).astype(jnp.bfloat16)
        pieces.append(
            jnp.einsum(
                "hqk,khd->qhd", probs_low, values[:block_end], preferred_element_type=jnp.float32
            )
        )
        log_totals.append(largest + jnp.log(denominator))
    return (
        jnp.concatenate(pieces, axis=0).astype(jnp.bfloat16),
        jnp.concatenate(log_totals, axis=1),
    )


def attend_backward(
    queries, key_rot, values, grad_attended, log_totals, segment, keep_mask, block_rows
):
    row_len = queries.shape[0]
    scaling = HEAD ** (-0.5)
    grad_queries = []
    grad_keys = jnp.zeros(key_rot.shape, jnp.float32)
    grad_values = jnp.zeros(values.shape, jnp.float32)
    for block_start in range(0, row_len, block_rows):
        block_end = block_start + block_rows
        masked = block_scores(queries, key_rot, segment, keep_mask, block_start, block_end)
        probs = jnp.exp(masked - log_totals[:, block_start:block_end])
        grad_probs = jnp.einsum(
            "qhd,khd->hqk",
            grad_attended[block_start:block_end],
            values[:block_end],
            preferred_element_type=jnp.float32,
        )
        centre = jnp.sum(probs * grad_probs, axis=-1, keepdims=True)
        grad_scores = (probs * (grad_probs - centre)).astype(jnp.bfloat16)
        grad_queries.append(
            jnp.einsum(
                "hqk,khd->qhd", grad_scores, key_rot[:block_end], preferred_element_type=jnp.float32
            )
            * scaling
        )
        padding = ((0, row_len - block_end), (0, 0), (0, 0))
        key_term = (
            jnp.einsum(
                "hqk,qhd->khd",
                grad_scores,
                queries[block_start:block_end],
                preferred_element_type=jnp.float32,
            )
            * scaling
        )
        value_term = jnp.einsum(
            "hqk,qhd->khd",
            probs.astype(jnp.bfloat16),
            grad_attended[block_start:block_end],
            preferred_element_type=jnp.float32,
        )
        grad_keys = grad_keys + jnp.pad(key_term, padding)
        grad_values = grad_values + jnp.pad(value_term, padding)
    return (jnp.concatenate(grad_queries, axis=0), grad_keys, grad_values)


def per_device(
    tokens,
    cotangent,
    lengths,
    pad_count,
    ln1_gain,
    ln1_bias,
    ln2_gain,
    ln2_bias,
    qkv_weight,
    qkv_bias,
    out_weight,
    out_bias,
    fc1_weight,
    fc1_bias,
    fc2_weight,
):
    local_tokens = tokens.shape[0]
    row_count = lengths.shape[0]
    row_len = local_tokens * lax.axis_size("mp") // row_count
    block_rows = min(512, row_len)
    width_here = qkv_weight.shape[2]
    heads_here = width_here // HEAD
    inputs = tokens.astype(jnp.float32)
    normed1 = layer_norm(inputs, ln1_gain, ln1_bias).astype(jnp.bfloat16)
    normed2 = layer_norm(inputs, ln2_gain, ln2_bias).astype(jnp.bfloat16)
    whole1, whole2 = (
        lax.all_gather(normed1, "mp", axis=0, tiled=True),
        lax.all_gather(normed2, "mp", axis=0, tiled=True),
    )
    saved, branch_rows, keep_rows = ([], [], [])
    row_index = 0
    segment, position, keep_mask = row_layout(lengths[row_index], pad_count[row_index], row_len)
    projected = (
        jnp.einsum("td,dce->cte", whole1, qkv_weight, preferred_element_type=jnp.float32)
        + qkv_bias[:, None, :]
    )
    queries = rotary(projected[0].reshape(row_len, heads_here, HEAD), position).astype(jnp.bfloat16)
    key_rot = rotary(projected[1].reshape(row_len, heads_here, HEAD), position).astype(jnp.bfloat16)
    values = projected[2].reshape(row_len, heads_here, HEAD).astype(jnp.bfloat16)
    attended, log_totals = attend_forward(queries, key_rot, values, segment, keep_mask, block_rows)
    attended = attended.reshape(row_len, width_here)
    pre_act = jnp.dot(whole2, fc1_weight, preferred_element_type=jnp.float32) + fc1_bias
    activated = exact_gelu(pre_act).astype(jnp.bfloat16)
    branch = jnp.dot(attended, out_weight, preferred_element_type=jnp.float32)
    branch = branch + jnp.dot(activated, fc2_weight, preferred_element_type=jnp.float32)
    branch_rows.append(branch)
    keep_rows.append(keep_mask)
    saved.append(
        (
            segment,
            position,
            keep_mask,
            queries,
            key_rot,
            values,
            log_totals,
            attended,
            pre_act,
            activated,
        )
    )
    summed = lax.psum_scatter(branch_rows[0], "mp", scatter_dimension=0, tiled=True)
    output = (inputs + summed + out_bias).astype(jnp.bfloat16)
    keep_all = keep_rows[0].astype(jnp.float32)
    keep_here = lax.dynamic_slice_in_dim(
        keep_all, lax.axis_index("mp") * local_tokens, local_tokens, 0
    )
    grad_out = cotangent.astype(jnp.float32) * keep_here[:, None]
    grad_whole = lax.all_gather(grad_out.astype(jnp.bfloat16), "mp", axis=0, tiled=True)
    grad_norm2_rows, grad_att_rows = ([], [])
    row_index = 0
    attended = saved[row_index][7]
    pre_act = saved[row_index][8]
    activated = saved[row_index][9]
    grad_fc2_w = jnp.einsum("tf,te->fe", activated, grad_whole, preferred_element_type=jnp.float32)
    grad_act = jnp.einsum("te,fe->tf", grad_whole, fc2_weight, preferred_element_type=jnp.float32)
    _, gelu_pull = jax.vjp(exact_gelu, pre_act)
    grad_pre = gelu_pull(grad_act)[0].astype(jnp.bfloat16)
    grad_fc1_w = jnp.einsum("td,tf->df", whole2, grad_pre, preferred_element_type=jnp.float32)
    grad_fc1_b = jnp.sum(grad_pre.astype(jnp.float32), axis=0)
    grad_norm2_rows.append(
        jnp.einsum("tf,df->td", grad_pre, fc1_weight, preferred_element_type=jnp.float32)
    )
    grad_out_w = jnp.einsum("tf,te->fe", attended, grad_whole, preferred_element_type=jnp.float32)
    grad_att_rows.append(
        jnp.einsum("te,fe->tf", grad_whole, out_weight, preferred_element_type=jnp.float32).astype(
            jnp.bfloat16
        )
    )
    row_index = 0
    segment, position, keep_mask, queries, key_rot, values, log_totals = saved[row_index][:7]
    grad_attended = grad_att_rows[row_index].reshape(row_len, heads_here, HEAD)
    grad_q, grad_k, grad_v = attend_backward(
        queries, key_rot, values, grad_attended, log_totals, segment, keep_mask, block_rows
    )
    _, rot_pull = jax.vjp(partial(rotary, position=position), jnp.zeros(grad_q.shape, jnp.float32))
    grad_projected = jnp.stack(
        [
            rot_pull(grad_q)[0].reshape(row_len, width_here),
            rot_pull(grad_k)[0].reshape(row_len, width_here),
            grad_v.reshape(row_len, width_here),
        ]
    ).astype(jnp.bfloat16)
    grad_qkv_w = jnp.einsum(
        "td,cte->dce", whole1, grad_projected, preferred_element_type=jnp.float32
    )
    grad_qkv_b = jnp.sum(grad_projected.astype(jnp.float32), axis=1)
    grad_norm1_rows = jnp.einsum(
        "cte,dce->td", grad_projected, qkv_weight, preferred_element_type=jnp.float32
    )
    grad_qkv_w, grad_qkv_b, grad_out_w, grad_fc1_w, grad_fc1_b, grad_fc2_w = lax.psum(
        (grad_qkv_w, grad_qkv_b, grad_out_w, grad_fc1_w, grad_fc1_b, grad_fc2_w), "dp"
    )
    grad_norm1, grad_norm2 = (
        lax.psum_scatter(grad_norm1_rows, "mp", scatter_dimension=0, tiled=True),
        lax.psum_scatter(grad_norm2_rows[0], "mp", scatter_dimension=0, tiled=True),
    )
    _, norm_pull1 = jax.vjp(layer_norm, inputs, ln1_gain, ln1_bias)
    grad_in1, grad_gain1, grad_shift1 = norm_pull1(grad_norm1)
    _, norm_pull2 = jax.vjp(layer_norm, inputs, ln2_gain, ln2_bias)
    grad_in2, grad_gain2, grad_shift2 = norm_pull2(grad_norm2)
    grad_tokens = grad_out + grad_in1 + grad_in2
    grad_gain1, grad_shift1, grad_gain2, grad_shift2, grad_bias_out = lax.psum(
        (grad_gain1, grad_shift1, grad_gain2, grad_shift2, jnp.sum(grad_out, axis=0)), ("dp", "mp")
    )
    return (
        output,
        grad_tokens,
        grad_gain1,
        grad_shift1,
        grad_gain2,
        grad_shift2,
        grad_qkv_w,
        grad_qkv_b,
        grad_out_w,
        grad_bias_out,
        grad_fc1_w,
        grad_fc1_b,
        grad_fc2_w,
    )


def solution(mesh):
    return jax.shard_map(
        per_device,
        mesh=mesh,
        in_specs=(
            P(("dp", "mp"), None),
            P(("dp", "mp"), None),
            P("dp", None),
            P("dp"),
            P(),
            P(),
            P(),
            P(),
            P(None, None, "mp"),
            P(None, "mp"),
            P("mp", None),
            P(),
            P(None, "mp"),
            P("mp"),
            P("mp", None),
        ),
        out_specs=(
            P(("dp", "mp"), None),
            P(("dp", "mp"), None),
            P(),
            P(),
            P(),
            P(),
            P(None, None, "mp"),
            P(None, "mp"),
            P("mp", None),
            P(),
            P(None, "mp"),
            P("mp"),
            P("mp", None),
        ),
        check_vma=False,
    )
```

profile of v0, /device:TPU:0, one launch (start us, length us, event | category | flops | bytes accessed | tf_op | source)
XLA Modules:
  0.0 1229.8 jit_solution(1869305157040266103)
XLA Ops:
  30.0 44.3 %all-gather.4.cloned.1.call-done = bf16[2048,1024]{1,0:T(8,128)(2,1)} async-done(((bf16[1024,1024]{1,0:T(8,128)(2,1)}), bf16[2048,1024]{1,0:T(8,128)(2,1)}) %all-gather.4.cloned.1.call-update) | async-done | bytes 4194320 | tf_op jit(solution)/shard_map/all_gather | solution.py:174
  74.2 11.9 fusion.125
  100.5 32.6 %all-gather.8.cloned.1.call-done = bf16[2048,1024]{1,0:T(8,128)(2,1)} async-done(((bf16[1024,1024]{1,0:T(8,128)(2,1)}), bf16[2048,1024]{1,0:T(8,128)(2,1)}) %all-gather.8.cloned.1.call-update) | async-done | bytes 4194320 | tf_op jit(solution)/shard_map/all_gather | solution.py:216
  172.5 11.4 multiply_reduce_fusion.2
  183.9 12.0 multiply_convert_fusion.2
  202.5 10.9 fusion.121
  213.4 11.3 fusion.2
  224.7 12.0 fusion.60
  236.7 16.1 %multiply_reduce_fusion.1 = (f32[8,512]{1,0:T(8,128)S(1)}, f32[8,512,1536]{2,1,0:T(8,128)}) fusion(f32[8,512,1536]{2,1,0:T(8,128)} %get-tuple-element.80, f32[8,512]{1,0:T(8,128)S(1)} %log_add_fusion.1, bf16[512,8,64]{0,2,1:T(8,128)(2,1)} %bitcast.140, bf16[1536,8,64]{0,2,1:T(8,128)(2,1)} %bitcast.137), kind=kOutput, calls=%fused_computation.9 | convolution fusion | flops 824176640 | bytes 52461568 | tf_op jit(solution)/shard_map/qhd,khd->hqk/dot_general | solution.py:112
  252.9 22.7 %multiply_convert_fusion.1 = bf16[8,512,1536]{2,1,0:T(8,128)(2,1)} fusion(f32[8,512,1536]{2,1,0:T(8,128)} %get-tuple-element.92, f32[8,512,1536]{2,1,0:T(8,128)} %get-tuple-element.80, f32[8,512]{1,0:T(8,128)S(1)} %get-tuple-element.91, f32[8,512]{1,0:T(8,128)S(1)} %log_add_fusion.1), kind=kLoop, calls=%fused_computation.8 | loop fusion | flops 25165824 | bytes 62947328 | tf_op jit(solution)/shard_map/convert_element_type | solution.py:119
  275.6 9.6 fusion.79
  293.8 14.0 %fusion.124 = (f32[8,512]{1,0:T(8,128)S(1)}, f32[8,512,2048]{2,1,0:T(8,128)}) fusion(bf16[512,8,64]{0,2,1:T(8,128)(2,1)S(1)} %copy-done.37, bf16[2048,8,16]{0,2,1:T(8,128)(2,1)S(1)} %copy-done.19, bf16[2048,8,48]{0,2,1:T(8,128)(2,1)S(1)} %copy-done.9, pred[512,2048]{1,0:T(8,128)(4,1)S(1)} %copy-done.52), kind=kOutput, calls=%fused_computation.225 | convolution fusion | flops 1103097856 | bytes 37240832 | tf_op jit(solution)/shard_map/qhd,khd->hqk/dot_general | solution.py:61
  307.9 13.8 %fusion = f32[8,512]{1,0:T(8,128)S(1)} fusion(f32[8,512,2048]{2,1,0:T(8,128)} %get-tuple-element.86, f32[8,512]{1,0:T(8,128)S(1)} %get-tuple-element.85), kind=kLoop, calls=%fused_computation.6 | loop fusion | flops 16773120 | bytes 33587200 | tf_op jit(solution)/shard_map/reduce_sum | solution.py:86
  321.8 22.2 %multiply_reduce_fusion = (f32[8,512]{1,0:T(8,128)S(1)}, f32[8,512,2048]{2,1,0:T(8,128)}) fusion(f32[8,512,2048]{2,1,0:T(8,128)} %get-tuple-element.86, f32[8,512]{1,0:T(8,128)S(1)} %log_add_fusion, bf16[512,8,64]{0,2,1:T(8,128)(2,1)S(1)} %bitcast.136, bf16[2048,8,64]{0,2,1:T(8,128)(2,1)S(1)} %bitcast.129), kind=kOutput, calls=%fused_computation.1 | convolution fusion | flops 1098903552 | bytes 69763072 | tf_op jit(solution)/shard_map/qhd,khd->hqk/dot_general | solution.py:112
  344.0 27.9 %multiply_convert_fusion = bf16[8,512,2048]{2,1,0:T(8,128)(2,1)} fusion(f32[8,512,2048]{2,1,0:T(8,128)} %get-tuple-element.90, f32[8,512,2048]{2,1,0:T(8,128)} %get-tuple-element.86, f32[8,512]{1,0:T(8,128)S(1)} %get-tuple-element.89, f32[8,512]{1,0:T(8,128)S(1)} %log_add_fusion), kind=kLoop, calls=%fused_computation | loop fusion | flops 33554432 | bytes 83918848 | tf_op jit(solution)/shard_map/convert_element_type | solution.py:119
  371.9 12.7 %fusion.77 = f32[512,8,64]{0,2,1:T(8,128)} fusion(bf16[8,512,2048]{2,1,0:T(8,128)(2,1)} %multiply_convert_fusion, bf16[2048,8,16]{0,2,1:T(8,128)(2,1)} %copy-done.18, bf16[2048,8,48]{0,2,1:T(8,128)(2,1)} %slice.348), kind=kOutput, calls=%fused_computation.143 | convolution fusion | flops 1078198272 | bytes 19922944 | tf_op jit(solution)/shard_map/hqk,khd->qhd/dot_general | solution.py:121
  384.6 10.8 bitcast_add_fusion.1
  402.0 16.5 %fusion.49 = bf16[2048,8,64]{0,2,1:T(8,128)(2,1)} fusion(f32[1536,8,64]{0,2,1:T(8,128)} %fusion.60, f32[1024,8,64]{0,2,1:T(8,128)} %fusion.69, f32[512,8,64]{0,2,1:T(8,128)} %fusion.73, bf16[512,8,64]{0,2,1:T(8,128)(2,1)} %bitcast.135, f32[8,512,2048]{2,1,0:T(8,128)} %get-tuple-element.86, f32[8,512]{1,0:T(8,128)S(1)} %log_add_fusion), kind=kOutput, calls=%fused_computation.92 | convolution fusion | flops 1094713344 | bytes 42483712 | tf_op jit(solution)/shard_map/hqk,qhd->khd/dot_general | solution.py:136
  440.4 10.8 convolution_bitcast_fusion
  451.9 49.6 %multiply_convert_fusion.3 = (bf16[2048,2048]{1,0:T(8,128)(2,1)}, f32[2048,2048]{1,0:T(8,128)}, f32[2048,2048]{1,0:T(8,128)}) fusion(f32[2048]{0:T(1024)S(1)} %copy-done.92, bf16[2048,1024]{1,0:T(8,128)(2,1)} %all-gather.6.cloned.1.call-done, bf16[1024,2048]{1,0:T(8,128)(2,1)} %param.27), kind=kOutput, calls=%fused_computation.25 | convolution fusion | flops 8866758656 | bytes 50339840 | tf_op jit(solution)/shard_map/dot_general | solution.py:189
  501.4 24.0 %convert_reduce_fusion = (f32[2048]{0:T(1024)}, bf16[2048,2048]{1,0:T(8,128)(2,1)}) fusion(f32[2048,2048]{1,0:T(8,128)} %get-tuple-element.37, bf16[2048,1024]{1,0:T(8,128)(2,1)} %all-gather.8.cloned.1.call-done, bf16[2048,1024]{1,0:T(8,128)(2,1)} %param.29, f32[2048,2048]{1,0:T(8,128)} %get-tuple-element.78, f32[2048]{0:T(1024)S(1)} %copy-done.92), kind=kOutput, calls=%fused_computation.19 | convolution fusion | flops 8661235712 | bytes 50348032 | tf_op jit(solution)/shard_map/te,fe->tf/dot_general | solution.py:223
  525.4 14.9 %fusion.127 = f32[2048,1024]{1,0:T(8,128)} fusion(bf16[2048,2048]{1,0:T(8,128)(2,1)} %get-tuple-element.98, bf16[1024,2048]{1,0:T(8,128)(2,1)} %param.27), kind=kOutput, calls=%fused_computation.228 | convolution fusion | flops 8589934592 | bytes 20971520 | tf_op jit(solution)/shard_map/tf,df->td/dot_general | solution.py:229
  547.3 13.7 %fusion.126 = f32[2048,1024]{1,0:T(8,128)} fusion(bf16[2048,2048]{1,0:T(8,128)(2,1)} %get-tuple-element.36, bf16[2048,1024]{1,0:T(8,128)(2,1)S(1)} %copy-done.88), kind=kOutput, calls=%fused_computation.227 | convolution fusion | flops 8589934592 | bytes 20971520 | tf_op jit(solution)/shard_map/dot_general | solution.py:192
  565.6 11.9 fusion.83
  577.6 15.1 %fusion.84 = bf16[8,64,512]{2,1,0:T(8,128)(2,1)} fusion(bf16[2048,8,64]{0,2,1:T(8,128)(2,1)S(1)} %bitcast.130, f32[8,512,2048]{2,1,0:T(8,128)} %get-tuple-element.86, f32[8,512]{1,0:T(8,128)S(1)} %copy-done.65, f32[8,512]{1,0:T(8,128)S(1)} %copy-done.63), kind=kOutput, calls=%fused_computation.153 | convolution fusion | flops 1099169792 | bytes 36208640 | tf_op jit(solution)/shard_map/hqk,khd->qhd/dot_general | solution.py:89
  592.7 9.9 convolution_add_fusion
  619.6 11.6 fusion.129
  631.3 11.6 fusion.128
  647.0 61.2 %all-reduce.15 = (f32[3,512]{1,0:T(4,128)}, f32[2048]{0:T(1024)}) all-reduce(f32[3,512]{1,0:T(4,128)S(1)} %convert_reduce_fusion.1, f32[2048]{0:T(1024)S(1)} %copy-done.84), channel_id=1, replica_groups=mesh['dp'=16,'mp'=2] {'dp'}, use_global_device_ids=true, to_apply=%region_34.35 | all-reduce | flops 3584 | bytes 28672 | tf_op jit(solution)/shard_map/psum | solution.py:258
  718.3 35.2 %reduce-scatter.4.cloned.1.call-done = f32[1024,1024]{1,0:T(8,128)} async-done(((f32[2048,1024]{1,0:T(8,128)}), f32[1024,1024]{1,0:T(8,128)}) %reduce-scatter.4.cloned.1.call-update) | async-done | bytes 4194320 | tf_op jit(solution)/shard_map/reduce_scatter | solution.py:209
  762.1 41.8 %all-reduce.14 = (f32[1024]{0:T(1024)}, f32[1024]{0:T(1024)}, f32[1024]{0:T(1024)}, f32[1024]{0:T(1024)}, f32[1024]{0:T(1024)}) all-reduce(f32[1024]{0:T(1024)S(1)} %get-tuple-element.22, f32[1024]{0:T(1024)S(1)} %get-tuple-element.19, f32[1024]{0:T(1024)S(1)} %get-tuple-element.13, ...), channel_id=1, replica_groups=mesh['dp'=16,'mp'=2] {'dp','mp'}, use_global_device_ids=true, to_apply=%region_25.26 | all-reduce | flops 5120 | bytes 40960 | tf_op jit(solution)/shard_map/psum | solution.py:270
  803.9 400.2 %all-reduce.19.cloned.1.call-done = (f32[1024,3,512]{2,0,1:T(8,128)}, f32[512,1024]{1,0:T(8,128)}, f32[1024,2048]{1,0:T(8,128)}, f32[2048,1024]{1,0:T(8,128)}) async-done(((f32[1024,3,512]{2,0,1:T(8,128)}, f32[512,1024]{1,0:T(8,128)}, f32[1024,2048]{1,0:T(8,128)}, f32[2048,1024]{1,0:T(8,128)}), (f32[1024,3,512]{2,0,1:T(8,128)}, f32[512,1024]{1,0:T(8,128)}, f32[1024,2048]{1,0:T(8,128)}, ...) | async-done | bytes 25165840 | tf_op jit(solution)/shard_map/psum | solution.py:258
  (313 shorter events, 189.3 us)
Async XLA Ops:
  7.2 67.1 %copy-start = (bf16[1024,3,512]{2,0,1:T(8,128)(2,1)S(1)}, bf16[1024,3,512]{2,0,1:T(8,128)(2,1)}, u32[]{:S(2)}) copy-start(bf16[1024,3,512]{2,0,1:T(8,128)(2,1)} %param.23) | copy-start | bytes 9437188
  7.2 67.0 %all-gather.4.cloned.1.call-start = ((), (), s32[]{:S(2)}) async-start(), calls=%async_computation.3 | async-start | bytes 6291456 | tf_op jit(solution)/shard_map/all_gather | solution.py:174
  14.6 118.5 %all-gather.8.cloned.1.call-start = ((), (), s32[]{:S(2)}) async-start(), calls=%async_computation.6 | async-start | bytes 6291456 | tf_op jit(solution)/shard_map/all_gather | solution.py:216
  19.3 54.9 %copy-start.91 = (f32[3,512]{1,0:T(4,128)S(1)}, f32[3,512]{1,0:T(4,128)}, u32[]{:S(2)}) copy-start(f32[3,512]{1,0:T(4,128)} %param.24) | copy-start | bytes 18436
  19.3 431.9 %all-gather.6.cloned.1.call-start = ((), (), s32[]{:S(2)}) async-start(), calls=%async_computation.4 | async-start | bytes 6291456 | tf_op jit(solution)/shard_map/all_gather | solution.py:175
  20.1 688.1 %reduce-scatter.6.cloned.1.call-start = ((), (), s32[]{:S(2)}) async-start(), calls=%async_computation.7 | async-start | bytes 12582912 | tf_op jit(solution)/shard_map/reduce_scatter | solution.py:262
  20.9 118.1 %copy-start.46 = (f32[2048,16]{0,1:T(8,128)}, f32[2048,16]{0,1:T(8,128)S(1)}, u32[]{:S(2)}) copy-start(f32[2048,16]{0,1:T(8,128)S(1)} %get-tuple-element.100) | copy-start | bytes 393220
  20.9 118.1 %copy-start.48 = (f32[2048,16]{0,1:T(8,128)}, f32[2048,16]{0,1:T(8,128)S(1)}, u32[]{:S(2)}) copy-start(f32[2048,16]{0,1:T(8,128)S(1)} %get-tuple-element.99) | copy-start | bytes 393220
  139.0 85.7 %copy-start.31 = (bf16[512,512]{0,1:T(8,128)(2,1)}, bf16[512,512]{0,1:T(8,128)(2,1)S(1)}, u32[]{:S(2)}) copy-start(bf16[512,512]{0,1:T(8,128)(2,1)S(1)} %get-tuple-element.52) | copy-start | bytes 1572868
  142.1 60.3 %copy-start.12 = (bf16[2048,8,16]{0,2,1:T(8,128)(2,1)}, bf16[2048,8,16]{0,2,1:T(8,128)(2,1)S(1)}, u32[]{:S(2)}) copy-start(bf16[2048,8,16]{0,2,1:T(8,128)(2,1)S(1)} %get-tuple-element.60) | copy-start | bytes 1572868
  142.1 60.3 %copy-start.18 = (bf16[2048,8,16]{0,2,1:T(8,128)(2,1)}, bf16[2048,8,16]{0,2,1:T(8,128)(2,1)S(1)}, u32[]{:S(2)}) copy-start(bf16[2048,8,16]{0,2,1:T(8,128)(2,1)S(1)} %get-tuple-element.59) | copy-start | bytes 1572868
  252.8 22.7 %copy-start.9 = (bf16[2048,8,48]{0,2,1:T(8,128)(2,1)S(1)}, bf16[2048,8,48]{0,2,1:T(8,128)(2,1)}, u32[]{:S(2)}) copy-start(bf16[2048,8,48]{0,2,1:T(8,128)(2,1)} %slice.348) | copy-start | bytes 4718596
  252.9 22.7 %copy-start.19 = (bf16[2048,8,16]{0,2,1:T(8,128)(2,1)S(1)}, bf16[2048,8,16]{0,2,1:T(8,128)(2,1)}, u32[]{:S(2)}) copy-start(bf16[2048,8,16]{0,2,1:T(8,128)(2,1)} %copy-done.18) | copy-start | bytes 1572868
  307.9 13.8 %copy-start.62 = (f32[8,512]{1,0:T(8,128)}, f32[8,512]{1,0:T(8,128)S(1)}, u32[]{:S(2)}) copy-start(f32[8,512]{1,0:T(8,128)S(1)} %get-tuple-element.85) | copy-start | bytes 49156
  307.9 13.9 %copy-start.26 = (bf16[1,2048,512]{1,2,0:T(8,128)(2,1)S(1)}, bf16[1,2048,512]{1,2,0:T(8,128)(2,1)}, u32[]{:S(2)}) copy-start(bf16[1,2048,512]{1,2,0:T(8,128)(2,1)} %slice.277) | copy-start | bytes 6291460
  307.9 13.9 %copy-start.29 = (bf16[512,512]{0,1:T(8,128)(2,1)S(1)}, bf16[512,512]{0,1:T(8,128)(2,1)}, u32[]{:S(2)}) copy-start(bf16[512,512]{0,1:T(8,128)(2,1)} %get-tuple-element.51) | copy-start | bytes 1572868
  321.7 22.2 %copy-start.64 = (f32[8,512]{1,0:T(8,128)}, f32[8,512]{1,0:T(8,128)S(1)}, u32[]{:S(2)}) copy-start(f32[8,512]{1,0:T(8,128)S(1)} %fusion) | copy-start | bytes 49156
  451.2 257.0 %reduce-scatter.8.cloned.1.call-start = ((), (), s32[]{:S(2)}) async-start(), calls=%async_computation.8 | async-start | bytes 12582912 | tf_op jit(solution)/shard_map/reduce_scatter | solution.py:263
  540.4 213.1 %reduce-scatter.4.cloned.1.call-start = ((), (), s32[]{:S(2)}) async-start(), calls=%async_computation.5 | async-start | bytes 12582912 | tf_op jit(solution)/shard_map/reduce_scatter | solution.py:209
  541.4 19.6 %slice-start = ((s8[16777216]{0:T(1024)(128)(4,1)}), s8[4194304]{0:T(1024)(128)(4,1)S(1)}, s32[]{:S(2)}) async-start(s8[16777216]{0:T(1024)(128)(4,1)} %bitcast.120), calls=%async_computation.10 | async-start | bytes 8388608
  541.4 19.6 %slice-start.1 = ((s8[16777216]{0:T(1024)(128)(4,1)}), s8[4194304]{0:T(1024)(128)(4,1)S(1)}, s32[]{:S(2)}) async-start(s8[16777216]{0:T(1024)(128)(4,1)} %bitcast.120), calls=%async_computation.11 | async-start | bytes 8388608
  547.3 13.7 %copy-start.61 = (f32[8,512]{1,0:T(8,128)S(1)}, f32[8,512]{1,0:T(8,128)}, u32[]{:S(2)}) copy-start(f32[8,512]{1,0:T(8,128)} %copy-done.60) | copy-start | bytes 49156
  577.6 15.1 %copy-start.50 = (bf16[512,1024]{1,0:T(8,128)(2,1)S(1)}, bf16[512,1024]{1,0:T(8,128)(2,1)}, u32[]{:S(2)}) copy-start(bf16[512,1024]{1,0:T(8,128)(2,1)} %param.25) | copy-start | bytes 3145732
  602.6 601.5 %all-reduce.19.cloned.1.call-start = ((), (), s32[]{:S(2)}) async-start(), calls=%async_computation.9 | async-start | bytes 50331648 | tf_op jit(solution)/shard_map/psum | solution.py:258
  603.8 15.8 %slice-start.9 = ((s8[8388608]{0:T(1024)(128)(4,1)}), s8[4194304]{0:T(1024)(128)(4,1)S(1)}, s32[]{:S(2)}) async-start(s8[8388608]{0:T(1024)(128)(4,1)} %bitcast.163), calls=%async_computation.19 | async-start | bytes 8388608
  610.2 21.1 %slice-start.7 = ((s8[8388608]{0:T(1024)(128)(4,1)}), s8[4194304]{0:T(1024)(128)(4,1)S(1)}, s32[]{:S(2)}) async-start(s8[8388608]{0:T(1024)(128)(4,1)} %bitcast.161), calls=%async_computation.17 | async-start | bytes 8388608
  642.9 65.3 %copy-start.7 = (bf16[1024,1024]{1,0:T(8,128)(2,1)S(1)}, bf16[1024,1024]{1,0:T(8,128)(2,1)}, u32[]{:S(2)}) copy-start(bf16[1024,1024]{1,0:T(8,128)(2,1)} %param.15) | copy-start | bytes 6291460
  642.9 65.3 %copy-start.57 = (f32[1024]{0:T(1024)S(1)}, f32[1024]{0:T(1024)}, u32[]{:S(2)}) copy-start(f32[1024]{0:T(1024)} %copy-done.56) | copy-start | bytes 12292
  642.9 65.3 %copy-start.67 = (f32[1024]{0:T(1024)S(1)}, f32[1024]{0:T(1024)}, u32[]{:S(2)}) copy-start(f32[1024]{0:T(1024)} %param.19) | copy-start | bytes 12292
  642.9 65.3 %copy-start.69 = (f32[1024]{0:T(1024)S(1)}, f32[1024]{0:T(1024)}, u32[]{:S(2)}) copy-start(f32[1024]{0:T(1024)} %param.21) | copy-start | bytes 12292
  714.3 39.2 %copy-start.81 = (f32[1024]{0:T(1024)S(1)}, f32[1024]{0:T(1024)}, u32[]{:S(2)}) copy-start(f32[1024]{0:T(1024)} %copy-done.80) | copy-start | bytes 12292
  714.3 39.2 %copy-start.87 = (f32[1024]{0:T(1024)S(1)}, f32[1024]{0:T(1024)}, u32[]{:S(2)}) copy-start(f32[1024]{0:T(1024)} %param.26) | copy-start | bytes 12292
  (80 other events, 454.3 us)
Sparse Core Ops, SparseCore 0:
  14.8 59.4 all-gather.3
  76.4 56.7 all-gather.7
  135.3 56.7 all-gather.5
  451.3 99.2 reduce-scatter.5
  552.8 99.2 reduce-scatter.7
  654.2 99.2 reduce-scatter.3
  760.3 443.7 all-reduce.18
where the time goes:
time: 1240 us; the launch traced here: 1230 us
  waiting for transfers between devices  513 us (41%)
  matrix products  385 us (31%)
  other arithmetic  155 us (12%)
  blocking collectives  103 us (8%)
  local copies, waits for them, and re-layouts  58 us (5%)
  between operations  16.1 us (1%)
    psum x1, waiting for transfers between devices, per_device(): lax.psum((grad_qkv_w, grad_qkv_b, grad_out_w, grad_fc1_w, grad_fc1_b, gra...  400 us
    convert_element_type x4, other arithmetic, attend_backward(): grad_scores = (probs * (grad_probs - centre)).astype(jnp.bfloat16)  65.4 us
    psum x1, blocking collectives, per_device(): lax.psum((grad_qkv_w, grad_qkv_b, grad_out_w, grad_fc1_w, grad_fc1_b, gra...  61.2 us
    dot_general x4, matrix products, attend_backward(): jnp.einsum('qhd,khd->hqk', grad_attended[block_start:block_end], values[:...  51.9 us
    dot_general x1, matrix products, per_device(): jnp.dot(whole2, fc1_weight, preferred_element_type=jnp.float32) + fc1_bias  49.6 us
    all_gather x1, waiting for transfers between devices, per_device(): lax.all_gather(normed1, 'mp', axis=0, tiled=True)  44.3 us
    psum x1, blocking collectives, per_device(): lax.psum((grad_gain1, grad_shift1, grad_gain2, grad_shift2, jnp.sum(grad_...  41.8 us
    dot_general x4, matrix products, attend_forward(): jnp.einsum('hqk,khd->qhd', probs_low, values[:block_end], preferred_eleme...  37.4 us
  transfers between devices with their start and end apart: 7, of which 4 were waited for; matrix products, arithmetic and copies ran while one was open for 45% of the time, Pallas kernels for 0%

commit v1 on v0

v1 whole, which is shorter than its diff:
```python
import functools

import jax
import jax.numpy as jnp
from jax import lax
from jax.experimental import pallas as pl
from jax.experimental.pallas import tpu as pltpu
from jax.sharding import PartitionSpec as P

HEAD = 64
ROT = 16
PAIR = 2 * HEAD
EPSILON = 1e-05
MASKED_SCORE = -1e30
ROTARY_BASE = 10000.0
SCALING = HEAD**-0.5
F32 = jnp.float32
BF16 = jnp.bfloat16
NN = ((1,), (0,))
NT = ((1,), (1,))
TN = ((0,), (0,))
MIB = 2**20


def dot(a, b, dims=NN):
    return lax.dot_general(a, b, (dims, ((), ())), preferred_element_type=F32)


def norm_stats(v):
    average = jnp.mean(v, axis=-1, keepdims=True)
    centred = v - average
    spread = jnp.mean(centred * centred, axis=-1, keepdims=True)
    return centred, lax.rsqrt(spread + EPSILON)


def turn(x, cosine, sine):
    half = ROT // 2
    u, w = x[:half], x[half:ROT]
    return jnp.concatenate([u * cosine - w * sine, w * cosine + u * sine, x[ROT:]], axis=0)


def project_body(place_ref, tok_ref, g_ref, gain_ref, shift_ref, w_ref, b_ref, wo_ref, cos_ref, sin_ref, *rest):
    q_out, kt_out, vt_out, k_out, v_out, n_out, do_out = rest[-7:]
    x = tok_ref[...].astype(F32)
    centred, rstd = norm_stats(x)
    normed = (centred * rstd * gain_ref[...] + shift_ref[...]).astype(BF16)
    n_out[...] = normed
    cosine, sine = cos_ref[...], sin_ref[...]
    width = wo_ref.shape[0]

    def head_rows(c, scale):
        p = dot(w_ref[c * width : (c + 1) * width, :], normed, NT) + b_ref[c * width : (c + 1) * width, :]
        if c == 2:
            return p.astype(BF16)
        parts = [turn(p[h : h + HEAD], cosine, sine) for h in range(0, width, HEAD)]
        return (jnp.concatenate(parts, axis=0) * scale).astype(BF16)

    q_out[...] = head_rows(0, SCALING)
    k = head_rows(1, 1.0)
    kt_out[...] = k
    k_out[...] = k.T
    v = head_rows(2, 1.0)
    vt_out[...] = v
    v_out[...] = v.T
    do_out[...] = dot(wo_ref[...], g_ref[...], NT).astype(BF16)


def project(place, tok, g, gain, shift, w_t, b_col, w_out, cosine, sine, row_len, before):
    half, d = tok.shape
    width = w_out.shape[0]
    rows = 256
    steps = half // rows
    here = lambda i, place: (i, 0)
    lanes = lambda i, place: (0, place[0] * steps + i)
    seq = lambda i, place: (place[0] * steps + i, 0)
    fixed = lambda i, place: (0, 0)
    specs = [
        pl.BlockSpec((rows, d), here),
        pl.BlockSpec((rows, d), here),
        pl.BlockSpec((1, d), fixed),
        pl.BlockSpec((1, d), fixed),
        pl.BlockSpec((3 * width, d), fixed),
        pl.BlockSpec((3 * width, 1), fixed),
        pl.BlockSpec((width, d), fixed),
        pl.BlockSpec((ROT // 2, rows), lanes),
        pl.BlockSpec((ROT // 2, rows), lanes),
    ]
    args = [place, tok, g, gain, shift, w_t, b_col, w_out, cosine, sine]
    aliases = {}
    if before is not None:
        specs += [pl.BlockSpec(memory_space=pl.ANY)] * 6
        aliases = {len(args) + i: i for i in range(6)}
        args += list(before)
    wide = jax.ShapeDtypeStruct((width, row_len), BF16)
    tall = jax.ShapeDtypeStruct((row_len, width), BF16)
    return pl.pallas_call(
        project_body,
        grid_spec=pltpu.PrefetchScalarGridSpec(
            num_scalar_prefetch=1,
            grid=(steps,),
            in_specs=specs,
            out_specs=[pl.BlockSpec((width, rows), lanes)] * 3
            + [pl.BlockSpec((rows, width), seq)] * 2
            + [pl.BlockSpec((rows, d), seq)]
            + [pl.BlockSpec((width, rows), lambda i, place: (0, i))],
        ),
        out_shape=[wide, wide, wide, tall, tall, jax.ShapeDtypeStruct((row_len, d), BF16), jax.ShapeDtypeStruct((width, half), BF16)],
        input_output_aliases=aliases,
        compiler_params=pltpu.CompilerParams(vmem_limit_bytes=40 * MIB),
        cost_estimate=pl.CostEstimate(flops=8 * half * d * width, bytes_accessed=16 * MIB, transcendentals=0),
        name="project",
    )(*args)


def gelu_parts(v):
    t = 1.0 / (1.0 + (0.3275911 * 0.7071067811865476) * jnp.abs(v))
    bell = jnp.exp(-0.5 * (v * v))
    poly = t * (0.127414796 + t * (-0.142248368 + t * (0.7107068705 + t * (-0.7265760135 + t * 0.5307027145))))
    tail = poly * bell
    below = jnp.where(v < 0.0, tail, 1.0 - tail)
    return v * below, below + v * (bell * 0.3989422804014327)


def mlp_body(*refs, first, rows):
    tok_ref, g_ref, gain_ref, shift_ref, w1_ref, b1_ref, w2_ref = refs[:7]
    refs = refs[7:]
    if not first:
        dw1_in, dw2_in = refs[:2]
        refs = refs[2:]
    out_ref, e_ref, dw1_ref, dw2_ref, db1_ref, dgain_ref, dshift_ref = refs[:7]
    normed, normed_t, out_acc, back_acc, act_t, pre_t = refs[7:]
    step = pl.program_id(0)
    last = pl.num_programs(0) - 1
    half, d = normed.shape
    blocks = half // rows

    @pl.when(step == 0)
    def _():
        def prepare(i, _):
            at = pl.ds(pl.multiple_of(i * rows, rows), rows)
            centred, rstd = norm_stats(tok_ref[at, :].astype(F32))
            n = (centred * rstd * gain_ref[...] + shift_ref[...]).astype(BF16)
            normed[at, :] = n
            normed_t[:, at] = n.T
            return 0

        lax.fori_loop(0, blocks, prepare, 0)
        dgain_ref[...] = jnp.zeros_like(dgain_ref)
        dshift_ref[...] = jnp.zeros_like(dshift_ref)

    def forward(i, bias_sum):
        at = pl.ds(pl.multiple_of(i * rows, rows), rows)
        v = dot(normed[at, :], w1_ref[...]) + b1_ref[...]
        grad_act = dot(g_ref[at, :], w2_ref[...], NT)
        act, slope = gelu_parts(v)
        act = act.astype(BF16)
        grad_pre = (grad_act * slope).astype(BF16)
        out = dot(act, w2_ref[...])
        back = dot(grad_pre, w1_ref[...], NT)

        @pl.when(step == 0)
        def _():
            out_acc[at, :] = out
            back_acc[at, :] = back

        @pl.when(step > 0)
        def _():
            out_acc[at, :] += out
            back_acc[at, :] += back

        act_t[:, at] = act.T
        pre_t[at, :] = grad_pre
        return bias_sum + jnp.sum(grad_pre.astype(F32), axis=0, keepdims=True)

    db1_ref[...] = lax.fori_loop(0, blocks, forward, jnp.zeros(db1_ref.shape, F32))

    def weights(i, _):
        at = pl.ds(pl.multiple_of(i * rows, rows), rows)
        one = dot(normed_t[at, :], pre_t[...])
        if not first:
            one = one + dw1_in[at, :].astype(F32)
        dw1_ref[at, :] = one.astype(BF16)
        two = dot(act_t[...], g_ref[:, at])
        if not first:
            two = two + dw2_in[:, at].astype(F32)
        dw2_ref[:, at] = two.astype(BF16)
        return 0

    for i in range(d // rows):
        weights(i, 0)

    @pl.when(step == last)
    def _():
        def finish(i, _):
            at = pl.ds(pl.multiple_of(i * rows, rows), rows)
            centred, rstd = norm_stats(tok_ref[at, :].astype(F32))
            back = back_acc[at, :]
            dgain_ref[...] += jnp.sum(back * (centred * rstd), axis=0, keepdims=True)
            dshift_ref[...] += jnp.sum(back, axis=0, keepdims=True)
            e_ref[at, :] = (back * gain_ref[...]).astype(BF16)
            out_ref[at, :] = out_acc[at, :].astype(BF16)
            return 0

        lax.fori_loop(0, blocks, finish, 0)


def mlp(tok, g, gain, shift, w1, b1, w2, before):
    half, d = tok.shape
    hidden = w1.shape[1]
    chunk = 512
    rows = 256
    fixed = lambda j: (0, 0)
    cols = pl.BlockSpec((d, chunk), lambda j: (0, j))
    tall = pl.BlockSpec((chunk, d), lambda j: (j, 0))
    whole = pl.BlockSpec((half, d), fixed)
    line = pl.BlockSpec((1, d), fixed)
    bias = pl.BlockSpec((1, chunk), lambda j: (0, j))
    args = [tok, g, gain, shift, w1, b1, w2]
    specs = [whole, whole, line, line, cols, bias, tall]
    if before is not None:
        args += list(before)
        specs += [cols, tall]
    shape = jax.ShapeDtypeStruct
    return pl.pallas_call(
        functools.partial(mlp_body, first=before is None, rows=rows),
        grid=(hidden // chunk,),
        in_specs=specs,
        out_specs=[whole, whole, cols, tall, bias, line, line],
        out_shape=[
            shape((half, d), BF16),
            shape((half, d), BF16),
            shape((d, hidden), BF16),
            shape((hidden, d), BF16),
            shape((1, hidden), F32),
            shape((1, d), F32),
            shape((1, d), F32),
        ],
        scratch_shapes=[
            pltpu.VMEM((half, d), BF16),
            pltpu.VMEM((d, half), BF16),
            pltpu.VMEM((half, d), F32),
            pltpu.VMEM((half, d), F32),
            pltpu.VMEM((chunk, half), BF16),
            pltpu.VMEM((half, chunk), BF16),
        ],
        compiler_params=pltpu.CompilerParams(vmem_limit_bytes=56 * MIB),
        cost_estimate=pl.CostEstimate(flops=12 * half * d * hidden, bytes_accessed=32 * MIB, transcendentals=0),
        name="feed_forward",
    )(*args)


def fold(x, op):
    return op(x.reshape(x.shape[0] // 8, 8, x.shape[1]), axis=0)


def attention_body(info_ref, q_ref, kt, vt, do_ref, k_ref, v_ref, start_ref, cosq_ref, sinq_ref, *rest, first, block):
    if first:
        o_ref, dq_ref, dk_ref, dv_ref, s_scr, e_scr = rest
    else:
        cos_ref, sin_ref, dq_in, dk_in, dv_in, o_ref, grads_ref, s_scr, e_scr, dk_ref, dv_ref = rest
    step = pl.program_id(1)
    half = pl.num_programs(1) * block
    place = info_ref[0] * pl.num_programs(1) + step
    row_len = kt.shape[1]

    @pl.when(step == 0)
    def _():
        if first:
            dk_ref[...] = jnp.zeros_like(dk_ref)
            dv_ref[...] = jnp.zeros_like(dv_ref)
        else:
            dk_ref[...] = dk_in[...]
            dv_ref[...] = dv_in[...]

    q_t = q_ref[...]
    zeros = jnp.zeros((HEAD, block), BF16)
    q_wide = [jnp.concatenate([q_t[:HEAD], zeros], 0), jnp.concatenate([zeros, q_t[HEAD:]], 0)]
    start = start_ref[...]
    spot = place * block + lax.broadcasted_iota(jnp.int32, (1, block), 1)
    low = info_ref[1 + step]
    high = place + 1
    rows = lax.broadcasted_iota(jnp.int32, (block, block // 2), 0)

    def scores(kb, tops):
        tops = list(tops)
        off = pl.multiple_of(kb * block, block)
        k_blk = k_ref[pl.ds(off, block), :]
        for w in range(2):
            at = slice(w * block // 2, (w + 1) * block // 2)
            legal = (rows >= start[:, at] - off) & (rows <= spot[:, at] - off)
            for h in range(2):
                s = jnp.where(legal, dot(k_blk, q_wide[h][:, at]), MASKED_SCORE)
                s_scr[h, pl.ds(off, block), at] = s
                tops[2 * h + w] = jnp.maximum(tops[2 * h + w], fold(s, jnp.max))
        return tuple(tops)

    tops = lax.fori_loop(low, high, scores, (jnp.full((8, block // 2), MASKED_SCORE, F32),) * 4)
    top = [jnp.max(jnp.concatenate(tops[2 * h : 2 * h + 2], 1), axis=0, keepdims=True) for h in range(2)]

    def forward(kb, carry):
        carry = list(carry)
        off = pl.multiple_of(kb * block, block)
        for h in range(2):
            e = jnp.exp(s_scr[h, pl.ds(off, block), :] - top[h])
            carry[h] = carry[h] + fold(e, jnp.sum)
            e = e.astype(BF16)
            e_scr[h, pl.ds(off, block), :] = e
            carry[2 + h] = carry[2 + h] + dot(vt[h * HEAD : (h + 1) * HEAD, pl.ds(off, block)], e)
        return tuple(carry)

    eight, tall = jnp.zeros((8, block), F32), jnp.zeros((HEAD, block), F32)
    sums = lax.fori_loop(low, high, forward, (eight, eight, tall, tall))
    grad = do_ref[...].astype(F32)
    centre, grad_low, grad_wide = [], [], []
    for h in range(2):
        at = slice(h * HEAD, (h + 1) * HEAD)
        inverse = 1.0 / jnp.sum(sums[h], axis=0, keepdims=True)
        o = sums[2 + h] * inverse
        o_ref[at, :] = o.astype(BF16)
        scaled = grad[at] * inverse
        centre.append(jnp.sum(scaled * o, axis=0, keepdims=True))
        grad_low.append(scaled.astype(BF16))
    grad_wide = [jnp.concatenate([grad_low[0], zeros], 0), jnp.concatenate([zeros, grad_low[1]], 0)]

    def backward(kb, carry):
        carry = list(carry)
        off = pl.multiple_of(kb * block, block)
        here = pl.ds(off, block)
        v_blk = v_ref[here, :]
        for h in range(2):
            at = slice(h * HEAD, (h + 1) * HEAD)
            e = e_scr[h, here, :]
            ds = (e.astype(F32) * (dot(v_blk, grad_wide[h]) - centre[h])).astype(BF16)
            dv_ref[at, here] += dot(grad_low[h], e, NT)
            dk_ref[at, here] += dot(q_t[at], ds, NT)
            carry[h] = carry[h] + dot(kt[at, here], ds)
        return tuple(carry)

    grads = lax.fori_loop(low, high, backward, (tall, tall))
    turned = [turn(grads[h] * SCALING, cosq_ref[...], -sinq_ref[...]).astype(BF16) for h in range(2)]
    if first:
        dq_ref[...] = jnp.concatenate(turned, 0)
    else:
        off = pl.multiple_of(place * block, block)
        grads_ref[0, :, pl.ds(off, block)] = jnp.concatenate(turned, 0)

        @pl.when(step == pl.num_programs(1) - 1)
        def _():
            other = pl.multiple_of((1 - info_ref[0]) * half, half)
            grads_ref[0, :, pl.ds(other, half)] = dq_in[...]

            def finish(i, _):
                here = pl.ds(pl.multiple_of(i * block, block), block)
                cosine, sine = cos_ref[:, here], -sin_ref[:, here]
                for h in range(2):
                    at = slice(h * HEAD, (h + 1) * HEAD)
                    grads_ref[1, at, here] = turn(dk_ref[at, here], cosine, sine).astype(BF16)
                grads_ref[2, :, here] = dv_ref[:, here].astype(BF16)
                return 0

            lax.fori_loop(0, row_len // block, finish, 0)


def attention(info, q_t, k_t, v_t, do_t, k, v, start, cosine, sine, before):
    width, row_len = q_t.shape
    half = do_t.shape[1]
    block = 512
    steps = half // block
    first = before is None
    place = lambda p, i, info: (p, info[0] * steps + i)
    line = lambda p, i, info: (0, info[0] * steps + i)
    here = pl.BlockSpec((PAIR, block), lambda p, i, info: (p, i))
    wide = pl.BlockSpec((PAIR, row_len), lambda p, i, info: (p, 0))
    tall = pl.BlockSpec((row_len, PAIR), lambda p, i, info: (0, p))
    angle = pl.BlockSpec((ROT // 2, block), line)
    args = [info, q_t, k_t, v_t, do_t, k, v, start, cosine, sine]
    specs = [pl.BlockSpec((PAIR, block), place), wide, wide, here, tall, tall, pl.BlockSpec((1, block), line), angle, angle]
    shape = jax.ShapeDtypeStruct
    scratch = [pltpu.VMEM((2, row_len, block), F32), pltpu.VMEM((2, row_len, block), BF16)]
    if first:
        outs = [shape((width, half), BF16)] * 2 + [shape((width, row_len), F32)] * 2
        out_specs = [here, here, wide, wide]
    else:
        table = pl.BlockSpec((ROT // 2, row_len), lambda p, i, info: (0, 0))
        args += [cosine, sine, *before]
        specs += [table, table, pl.BlockSpec((PAIR, half), lambda p, i, info: (p, 0)), wide, wide]
        outs = [shape((width, half), BF16), shape((3, width, row_len), BF16)]
        out_specs = [here, pl.BlockSpec((3, PAIR, row_len), lambda p, i, info: (0, p, 0))]
        scratch += [pltpu.VMEM((PAIR, row_len), F32)] * 2
    return pl.pallas_call(
        functools.partial(attention_body, first=first, block=block),
        grid_spec=pltpu.PrefetchScalarGridSpec(
            num_scalar_prefetch=1,
            grid=(width // PAIR, steps),
            in_specs=specs,
            out_specs=out_specs,
            scratch_shapes=scratch,
        ),
        out_shape=outs,
        compiler_params=pltpu.CompilerParams(vmem_limit_bytes=48 * MIB),
        cost_estimate=pl.CostEstimate(flops=24 * half * half * width * 2, bytes_accessed=16 * MIB, transcendentals=0),
        name="attention",
    )(*args)


def per_device(
    tokens,
    cotangent,
    lengths,
    pad_count,
    ln1_gain,
    ln1_bias,
    ln2_gain,
    ln2_bias,
    qkv_weight,
    qkv_bias,
    out_weight,
    out_bias,
    fc1_weight,
    fc1_bias,
    fc2_weight,
):
    half, d = tokens.shape
    row_len = half * lax.axis_size("mp")
    width = qkv_weight.shape[2]
    me = lax.axis_index("mp")
    swap = [(0, 1), (1, 0)]
    tok_far = lax.ppermute(tokens, "mp", swap)
    cot_later, tok_far = lax.optimization_barrier((cotangent, tok_far))
    cot_far = lax.ppermute(cot_later, "mp", swap)

    docs = lengths.shape[1]
    order = jnp.arange(docs)
    starts = jnp.sum(jnp.where(order[None, :] < order[:, None], lengths[0][None, :], 0), axis=1)
    places = jnp.arange(row_len, dtype=jnp.int32)
    doc_start = jnp.max(jnp.where(starts[:, None] <= places[None, :], starts[:, None], 0), axis=0)
    kept = row_len - pad_count[0]
    start = jnp.where(places < kept, doc_start, places).astype(jnp.int32)
    frequency = ROTARY_BASE ** (-(jnp.arange(ROT // 2, dtype=F32) * 2.0) / ROT)
    angles = frequency[:, None] * (places - doc_start).astype(F32)[None, :]
    cosine, sine = jnp.cos(angles), jnp.sin(angles)
    block = 512
    lows = (start[::block] // block).astype(jnp.int32).reshape(2, -1)
    near = jnp.concatenate([me[None].astype(jnp.int32), lows[me]])
    far = jnp.concatenate([(1 - me)[None].astype(jnp.int32), lows[1 - me]])

    inside = jnp.arange(half, dtype=jnp.int32)[:, None]
    g_near = jnp.where(inside < kept - me * half, cotangent, jnp.zeros((), BF16))
    g_far = jnp.where(inside < kept - (1 - me) * half, cot_far, jnp.zeros((), BF16))

    gain1, shift1 = ln1_gain[None], ln1_bias[None]
    gain2, shift2 = ln2_gain[None], ln2_bias[None]
    w_t = jnp.transpose(qkv_weight, (1, 2, 0)).reshape(3 * width, d)
    b_col = qkv_bias.reshape(3 * width, 1)
    b1 = fc1_bias[None]

    mlp_near = mlp(tokens, g_near, gain2, shift2, fc1_weight, b1, fc2_weight, None)
    front = (gain1, shift1, w_t, b_col, out_weight, cosine, sine, row_len)
    *made, do_near = project(near[:1], tokens, g_near, *front, None)
    q_t, k_t, v_t, k, v, normed1, do_far = project(far[:1], tok_far, g_far, *front, made)
    o_near, dq_near, dk, dv = attention(near, q_t, k_t, v_t, do_near, k, v, start[None], cosine, sine, None)
    mlp_far = mlp(tok_far, g_far, gain2, shift2, fc1_weight, b1, fc2_weight, mlp_near[2:4])
    grad_fc1 = lax.psum(mlp_far[2], "dp")
    grad_fc2 = lax.psum(mlp_far[3], "dp")
    o_far, grads = attention(far, q_t, k_t, v_t, do_far, k, v, start[None], cosine, sine, (dq_near, dk, dv))

    branch_far = dot(o_far, out_weight, TN) + mlp_far[0].astype(F32)
    arrived = lax.ppermute(branch_far.astype(BF16), "mp", swap)
    branch = dot(o_near, out_weight, TN) + mlp_near[0].astype(F32)
    output = (tokens.astype(F32) + (branch + arrived.astype(F32)) + out_bias).astype(BF16)

    grads = grads.reshape(3 * width, row_len)
    grad_qkv = dot(grads, normed1).astype(BF16)
    grad_out_w = (dot(o_near, g_near) + dot(o_far, g_far)).astype(BF16)
    grad_qkv = lax.psum(grad_qkv, "dp")
    grad_out_w = lax.psum(grad_out_w, "dp")
    grad_qkv_b = jnp.sum(grads.astype(F32), axis=1)

    def norm_back(place, tok, e2):
        part = lax.dynamic_slice_in_dim(grads, place * half, half, 1)
        back = dot(part, w_t, TN)
        centred, rstd = norm_stats(tok.astype(F32))
        xhat = centred * rstd
        return gain1 * back + e2.astype(F32), jnp.sum(back * xhat, axis=0), jnp.sum(back, axis=0)

    e_far, dgain_far, dshift_far = norm_back(1 - me, tok_far, mlp_far[1])
    e_arrived = lax.ppermute(e_far.astype(BF16), "mp", swap)
    e_near, dgain_near, dshift_near = norm_back(me, tokens, mlp_near[1])
    e = e_near + e_arrived.astype(F32)
    centred, rstd = norm_stats(tokens.astype(F32))
    xhat = centred * rstd
    grad_in = rstd * (e - jnp.mean(e, axis=-1, keepdims=True) - xhat * jnp.mean(e * xhat, axis=-1, keepdims=True))
    g_wide = g_near.astype(F32)
    grad_tokens = g_wide + grad_in

    both = jnp.stack(
        [
            dgain_near + dgain_far,
            dshift_near + dshift_far,
            (mlp_near[5] + mlp_far[5])[0],
            (mlp_near[6] + mlp_far[6])[0],
            jnp.sum(g_wide, axis=0),
        ]
    )
    both = both + lax.ppermute(both, "mp", swap)
    small = jnp.concatenate([both.reshape(-1), grad_qkv_b, (mlp_near[4] + mlp_far[4])[0]])
    small = lax.psum(small, "dp")
    both = small[: 5 * d].reshape(5, d)
    grad_qkv_b = small[5 * d : 5 * d + 3 * width].reshape(3, width)
    grad_fc1_b = small[5 * d + 3 * width :]
    return (
        output,
        grad_tokens,
        both[0],
        both[1],
        both[2],
        both[3],
        jnp.transpose(grad_qkv.reshape(3, width, d), (2, 0, 1)).astype(F32),
        grad_qkv_b,
        grad_out_w.astype(F32),
        both[4],
        grad_fc1.astype(F32),
        grad_fc1_b,
        grad_fc2.astype(F32),
    )


def solution(mesh):
    return jax.shard_map(
        per_device,
        mesh=mesh,
        in_specs=(
            P(("dp", "mp"), None),
            P(("dp", "mp"), None),
            P("dp", None),
            P("dp"),
            P(),
            P(),
            P(),
            P(),
            P(None, None, "mp"),
            P(None, "mp"),
            P("mp", None),
            P(),
            P(None, "mp"),
            P("mp"),
            P("mp", None),
        ),
        out_specs=(
            P(("dp", "mp"), None),
            P(("dp", "mp"), None),
            P(),
            P(),
            P(),
            P(),
            P(None, None, "mp"),
            P(None, "mp"),
            P("mp", None),
            P(),
            P(None, "mp"),
            P("mp"),
            P("mp", None),
        ),
        check_vma=False,
    )
```

time: 1240 us -> 575 us (0.46)
  matrix products: 385 us -> 29.9 us
  waiting for transfers between devices: 513 us -> 164 us
  Pallas kernels: 0 us -> 206 us
  other arithmetic: 155 us -> 51.6 us
  local copies, waits for them, and re-layouts: 58 us -> 18.1 us
  blocking collectives: 103 us -> 75.6 us
    dot_general x36 -> x7, matrix products: 385 us -> 29.9 us  [dot(): return lax.dot_general(a, b, (dims, ((), ())), preferred_element_type=F32)]
    psum x1, waiting for transfers between devices: 400 us -> 73.8 us  [per_device(): grad_qkv = lax.psum(grad_qkv, 'dp')]
    pallas_call x0 -> x6, Pallas kernels: none -> 206 us  [the longest x2 99.2 us: mlp(): pl.pallas_call(functools.partial(mlp_body, first=before is None, rows=row...]
    ppermute x0 -> x5, waiting for transfers between devices: none -> 90.5 us  [the longest x1 44.9 us: per_device(): arrived = lax.ppermute(branch_far.astype(BF16), 'mp', swap)]
    all_gather x3 -> x0, waiting for transfers between devices: 76.9 us -> none  [the longest x1 44.3 us: per_device(): lax.all_gather(normed1, 'mp', axis=0, tiled=True)]
    convert_element_type x8 -> x6, other arithmetic: 71.5 us -> 18.2 us  [the longest x1 5.64 us: per_device(): jnp.transpose(grad_qkv.reshape(3, width, d), (2, 0, 1)).astype(F32)]
    reduce_scatter x3 -> x0, waiting for transfers between devices: 35.3 us -> none  [the longest x1 35.2 us: per_device(): lax.psum_scatter(branch_rows[0], 'mp', scatter_dimension=0, tiled=True)]
    reduce_sum x12 -> x9, other arithmetic: 55.7 us -> 26.1 us  [the longest x2 11.4 us: norm_back(): jnp.sum(back, axis=0)]
  transfers between devices with their start and end apart: 7 -> 6, of which waited for: 4 -> 4; matrix products, arithmetic and copies ran while one was open for 45% -> 10% of each run, Pallas kernels for 0% -> 10%
where the time goes in v1:
time: 575 us; the launch traced here: 566 us
  Pallas kernels  206 us (36%)
  waiting for transfers between devices  164 us (29%)
  blocking collectives  75.6 us (13%)
  other arithmetic  51.6 us (9%)
  matrix products  29.9 us (5%)
  local copies, waits for them, and re-layouts  18.1 us (3%)
  between operations  15.6 us (3%)
    pallas_call x2, Pallas kernels, mlp(): pl.pallas_call(functools.partial(mlp_body, first=before is None, rows=row...  99.2 us
    pallas_call x2, Pallas kernels, attention(): pl.pallas_call(functools.partial(attention_body, first=first, block=block...  85.7 us
    psum x1, blocking collectives, per_device(): small = lax.psum(small, 'dp')  75.6 us
    psum x1, waiting for transfers between devices, per_device(): grad_qkv = lax.psum(grad_qkv, 'dp')  73.8 us
    ppermute x1, waiting for transfers between devices, per_device(): arrived = lax.ppermute(branch_far.astype(BF16), 'mp', swap)  44.9 us
    ppermute x1, waiting for transfers between devices, per_device(): cot_far = lax.ppermute(cot_later, 'mp', swap)  32.1 us
    dot_general x7, matrix products, dot(): return lax.dot_general(a, b, (dims, ((), ())), preferred_element_type=F32)  29.9 us
    pallas_call x2, Pallas kernels, project(): pl.pallas_call(project_body, grid_spec=pltpu.PrefetchScalarGridSpec(num_s...  20.9 us
  transfers between devices with their start and end apart: 6, of which 4 were waited for; matrix products, arithmetic and copies ran while one was open for 10% of the time, Pallas kernels for 10%

profile of v1, /device:TPU:0, one launch (start us, length us, event | category | flops | bytes accessed | tf_op | source)
XLA Modules:
  0.0 566.3 jit_solution(3491033396091217235)
XLA Ops:
  7.2 3.0 collective-permute-start
  10.3 4.6 copy.40
  16.6 4.1 convert_reduce_fusion.3
  20.8 48.8 %feed_forward.2 = (bf16[1024,1024]{1,0:T(8,128)(2,1)}, bf16[1024,1024]{1,0:T(8,128)(2,1)}, bf16[1024,2048]{1,0:T(8,128)(2,1)}, bf16[2048,1024]{1,0:T(8,128)(2,1)...) custom-call(bf16[1024,1024]{1,0:T(8,128)(2,1)} %refs_0_.1, ...), custom_call_target="tpu_custom_call" | custom-call | flops 25769803776 | bytes 33554432 | tf_op jit(solution)/shard_map/feed_forward/pallas_call | solution.py:224
  70.1 10.5 %project.2 = (bf16[512,2048]{1,0:T(8,128)(2,1)S(1)}, bf16[512,2048]{1,0:T(8,128)(2,1)S(1)}, bf16[512,2048]{1,0:T(8,128)(2,1)S(1)}, bf16[2048,512]{1,0:T(8,128)(2...) custom-call(s32[1]{0:T(128)} %bitcast.place_ref, ...), custom_call_target="tpu_custom_call" | custom-call | flops 4294967296 | bytes 16777216 | tf_op jit(solution)/shard_map/project/pallas_call | solution.py:96
  80.6 1.9 convert_reduce_fusion.2
  82.5 2.3 fusion.12
  84.8 32.1 %collective-permute-done.1 = bf16[1024,1024]{1,0:T(8,128)(2,1)S(1)} collective-permute-done((bf16[1024,1024]{1,0:T(8,128)(2,1)}, bf16[1024,1024]{1,0:T(8,128)(2,1)S(1)}, u32[]{:S(2)}, u32[]{:S(2)}) %collective-permute-start.1) | collective-permute-done | bytes 2097184 | tf_op jit(solution)/shard_map/ppermute | solution.py:430
  118.5 10.4 %project.3 = (bf16[512,2048]{1,0:T(8,128)(2,1)S(1)}, bf16[512,2048]{1,0:T(8,128)(2,1)S(1)}, bf16[512,2048]{1,0:T(8,128)(2,1)S(1)}, bf16[2048,512]{1,0:T(8,128)(2...) custom-call(s32[1]{0:T(128)} %bitcast.4.place_ref, ...), custom_call_target="tpu_custom_call", output_to_operand_aliasing={{0}: (10, {}), {1}: (11, {}), {2}: (12, {}), {3}: (13, {}),... | custom-call | flops 4294967296 | bytes 16777216 | tf_op jit(solution)/shard_map/project/pallas_call | solution.py:96
  134.2 33.3 %attention.2 = (bf16[512,1024]{1,0:T(8,128)(2,1)S(1)}, bf16[512,1024]{1,0:T(8,128)(2,1)S(1)}, f32[512,2048]{1,0:T(8,128)}, f32[512,2048]{1,0:T(8,128)}) custom-call(s32[3]{0:T(128)S(1)} %get-tuple-element.114.info_ref, bf16[512,2048]{1,0:T(8,128)(2,1)S(1)} %get-tuple-element.57.q_ref, bf16[512,2048]{1,0:T(8,128)(2,1)} %copy-done.1, ...), custom_call_target="tpu_custom_call" | custom-call | flops 25769803776 | bytes 16777216 | tf_op jit(solution)/shard_map/attention/pallas_call | solution.py:390
  167.5 52.4 %attention.3 = (bf16[512,1024]{1,0:T(8,128)(2,1)S(1)}, bf16[3,512,2048]{2,1,0:T(8,128)(2,1)}) custom-call(s32[3]{0:T(128)S(1)} %get-tuple-element.115.info_ref, bf16[512,2048]{1,0:T(8,128)(2,1)S(1)} %get-tuple-element.57.q_ref, bf16[512,2048]{1,0:T(8,128)(2,1)} %copy-done.1, bf16[512,2048]{1,0:T(8,128)(2,1)} %copy-done.2, ...), custom_call_target="tpu_custom_call" | custom-call | flops 25769803776 | bytes 16777216 | tf_op jit(solution)/shard_map/attention/pallas_call | solution.py:390
  220.0 10.0 %convolution_convert_fusion = bf16[1536,1024]{1,0:T(8,128)(2,1)} fusion(bf16[1536,2048]{1,0:T(8,128)(2,1)} %bitcast.50, bf16[2048,1024]{1,0:T(8,128)(2,1)S(1)} %copy-done.13), kind=kOutput, calls=%fused_computation.28 | convolution fusion | flops 6444023808 | bytes 13631488 | tf_op jit(solution)/shard_map/dot_general | solution.py:26
  229.9 4.7 copy.43
  234.6 2.9 fusion.31
  237.5 50.4 %feed_forward.3 = (bf16[1024,1024]{1,0:T(8,128)(2,1)}, bf16[1024,1024]{1,0:T(8,128)(2,1)}, bf16[1024,2048]{1,0:T(8,128)(2,1)}, bf16[2048,1024]{1,0:T(8,128)(2,1)...) custom-call(bf16[1024,1024]{1,0:T(8,128)(2,1)} %collective-permute-done.tok_ref.refs_0_, ...), custom_call_target="tpu_custom_call" | custom-call | flops 25769803776 | bytes 33554432 | tf_op jit(solution)/shard_map/feed_forward/pallas_call | solution.py:224
  287.9 2.3 add_convert_fusion.2
  290.2 6.6 %fusion.17 = f32[1024,1024]{1,0:T(8,128)S(1)} fusion(bf16[1536,1024]{1,0:T(8,128)(2,1)} %bitcast.47, bf16[1536,2048]{1,0:T(8,128)(2,1)} %bitcast.51, s32[]{:T(128)S(6)} %select_n.55), kind=kOutput, calls=%fused_computation.29 | convolution fusion | flops 3221225472 | bytes 10485764 | tf_op jit(solution)/shard_map/dot_general | solution.py:26
  296.8 4.0 fusion.25
  302.5 2.1 add_convert_fusion.1
  304.6 1.7 collective-permute-start.2
  306.4 2.3 fusion.11
  308.7 3.7 convert_reduce_fusion
  314.8 5.6 fusion.19
  320.5 13.5 %collective-permute-done.3 = bf16[1024,1024]{1,0:T(8,128)(2,1)} collective-permute-done((bf16[1024,1024]{1,0:T(8,128)(2,1)}, bf16[1024,1024]{1,0:T(8,128)(2,1)}, u32[]{:S(2)}, u32[]{:S(2)}) %collective-permute-start.3) | collective-permute-done | bytes 2097184 | tf_op jit(solution)/shard_map/ppermute | solution.py:487
  334.0 44.9 %collective-permute-done.2 = bf16[1024,1024]{1,0:T(8,128)(2,1)} collective-permute-done((bf16[1024,1024]{1,0:T(8,128)(2,1)}, bf16[1024,1024]{1,0:T(8,128)(2,1)}, u32[]{:S(2)}, u32[]{:S(2)}) %collective-permute-start.2) | collective-permute-done | bytes 2097184 | tf_op jit(solution)/shard_map/ppermute | solution.py:468
  378.9 7.4 %fusion.26 = (f32[1024]{0:T(1024)S(1)}, f32[1024]{0:T(1024)S(1)}, f32[1024]{0:T(1024)S(1)}, f32[1024]{0:T(1024)S(1)}, f32[1024,1024]{1,0:T(8,128)}, /*index=5*/bf16[1024,1024]{1,0:T(8,128)(2,1)}) fusion(f32[1024,1024]{1,0:T(8,128)S(1)} %fusion.19, f32[1024]{0:T(1024)S(1)} %add_rsqrt_fusion.1, f32[1024]{0:T(1024)S(1)} %broadcast_multiply_fusion.3, ...), kind=kLoop, calls=%fused_computation.69 | loop fusion | flops 22016000 | bytes 25198592 | tf_op jit(solution)/shard_map/reduce_sum | solution.py:484
  386.5 5.1 convert_add_fusion.1
  391.6 75.6 %psum.35 = f32[8704]{0:T(1024)S(1)} all-reduce(f32[8704]{0:T(1024)S(1)} %pad_maximum_fusion), channel_id=1, replica_groups=mesh['dp'=16,'mp'=2] {'dp'}, use_global_device_ids=true, to_apply=%region_14.15 | all-reduce | flops 8704 | bytes 69632 | tf_op jit(solution)/shard_map/psum | solution.py:507
  469.1 73.8 %all-reduce.3.cloned.1.call-done = (bf16[1024,3,512]{2,0,1:T(8,128)(2,1)}, bf16[512,1024]{1,0:T(8,128)(2,1)}, bf16[1024,2048]{1,0:T(8,128)(2,1)}, bf16[2048,1024]{1,0:T(8,128)(2,1)}) async-done(((bf16[1024,3,512]{2,0,1:T(8,128)(2,1)}, bf16[512,1024]{1,0:T(8,128)(2,1)}, bf16[1024,2048]{1,0:T(8,128)(2,1)}, bf16[2048,1024]{1,0:T(8,128)(2,1)}), (bf16[1024,3,512]{2,0,1:T(8,128)(2,1)}, ...) | async-done | bytes 12582928 | tf_op jit(solution)/shard_map/psum | solution.py:475
  542.9 5.6 convert_element_type.90
  550.1 4.5 convert_element_type.93
  554.5 4.4 convert_element_type.94
  (105 shorter events, 16.2 us)
Async XLA Ops:
  7.2 7.7 %copy-start.28 = (s32[1,8]{1,0:T(1,128)S(1)}, s32[1,8]{1,0:T(1,128)}, u32[]{:S(2)}) copy-start(s32[1,8]{1,0:T(1,128)} %param.17) | copy-start | bytes 100
  7.2 8.8 %copy-start.22 = (f32[3,512]{1,0:T(4,128)S(1)}, f32[3,512]{1,0:T(4,128)}, u32[]{:S(2)}) copy-start(f32[3,512]{1,0:T(4,128)} %param.24) | copy-start | bytes 18436
  7.2 535.7 %all-reduce.3.cloned.1.call-start = ((), (), s32[]{:S(2)}) async-start(), calls=%async_computation | async-start | bytes 25165824 | tf_op jit(solution)/shard_map/psum | solution.py:475
  7.2 62.3 %collective-permute-start = (bf16[1024,1024]{1,0:T(8,128)(2,1)}, bf16[1024,1024]{1,0:T(8,128)(2,1)}, u32[]{:S(2)}, u32[]{:S(2)}) collective-permute-start(bf16[1024,1024]{1,0:T(8,128)(2,1)} %refs_0_.1), channel_id=1, source_target_pairs={{0,1},{1,0},{2,3},{3,2},{4,5},{5,4},{6,7},{7,6},{8,9},{9,8},{10,11... | collective-permute-start | bytes 6291464 | tf_op jit(solution)/shard_map/ppermute | solution.py:428
  20.7 49.0 %copy-start.7 = (bf16[1024,1024]{1,0:T(8,128)(2,1)S(1)}, bf16[1024,1024]{1,0:T(8,128)(2,1)}, u32[]{:S(2)}) copy-start(bf16[1024,1024]{1,0:T(8,128)(2,1)} %refs_0_.1) | copy-start | bytes 6291460
  20.7 49.4 %copy-start = (bf16[512,1024]{1,0:T(8,128)(2,1)S(1)}, bf16[512,1024]{1,0:T(8,128)(2,1)}, u32[]{:S(2)}) copy-start(bf16[512,1024]{1,0:T(8,128)(2,1)} %wo_ref.3) | copy-start | bytes 3145732
  20.7 49.4 %copy-start.5 = (f32[1024]{0:T(1024)S(1)}, f32[1024]{0:T(1024)}, u32[]{:S(2)}) copy-start(f32[1024]{0:T(1024)} %param.19) | copy-start | bytes 12292
  20.7 49.4 %copy-start.6 = (f32[1024]{0:T(1024)S(1)}, f32[1024]{0:T(1024)}, u32[]{:S(2)}) copy-start(f32[1024]{0:T(1024)} %param.20) | copy-start | bytes 12292
  69.6 47.4 %collective-permute-start.1 = (bf16[1024,1024]{1,0:T(8,128)(2,1)}, bf16[1024,1024]{1,0:T(8,128)(2,1)S(1)}, u32[]{:S(2)}, u32[]{:S(2)}) collective-permute-start(bf16[1024,1024]{1,0:T(8,128)(2,1)} %param.16), channel_id=1, source_target_pairs={{0,1},{1,0},{2,3},{3,2},{4,5},{5,4},{6,7},{7,6},{8,9},{9,8},{10,11... | collective-permute-start | bytes 6291464 | tf_op jit(solution)/shard_map/ppermute | solution.py:430
  130.2 1.4 copy-start.2
  167.5 52.4 %copy-start.13 = (bf16[2048,1024]{1,0:T(8,128)(2,1)S(1)}, bf16[2048,1024]{1,0:T(8,128)(2,1)}, u32[]{:S(2)}) copy-start(bf16[2048,1024]{1,0:T(8,128)(2,1)} %get-tuple-element.82) | copy-start | bytes 12582916
  237.4 50.4 %copy-start.10 = (bf16[1024,1024]{1,0:T(8,128)(2,1)S(1)}, bf16[1024,1024]{1,0:T(8,128)(2,1)}, u32[]{:S(2)}) copy-start(bf16[1024,1024]{1,0:T(8,128)(2,1)} %broadcast_select_fusion.1.g_ref.refs_1_) | copy-start | bytes 6291460
  290.2 6.6 %copy-start.16 = (bf16[1024,1024]{1,0:T(8,128)(2,1)S(1)}, bf16[1024,1024]{1,0:T(8,128)(2,1)}, u32[]{:S(2)}) copy-start(bf16[1024,1024]{1,0:T(8,128)(2,1)} %get-tuple-element.75) | copy-start | bytes 6291460
  300.8 1.7 copy-start.17
  300.8 33.1 %collective-permute-start.3 = (bf16[1024,1024]{1,0:T(8,128)(2,1)}, bf16[1024,1024]{1,0:T(8,128)(2,1)}, u32[]{:S(2)}, u32[]{:S(2)}) collective-permute-start(bf16[1024,1024]{1,0:T(8,128)(2,1)} %get-tuple-element.101), channel_id=1, source_target_pairs={{0,1},{1,0},{2,3},{3,2},{4,5},{5,4},{6,7},{7,6},{8,9},{9,8},{10,11... | collective-permute-start | bytes 6291464 | tf_op jit(solution)/shard_map/ppermute | solution.py:487
  304.6 74.3 %collective-permute-start.2 = (bf16[1024,1024]{1,0:T(8,128)(2,1)}, bf16[1024,1024]{1,0:T(8,128)(2,1)}, u32[]{:S(2)}, u32[]{:S(2)}) collective-permute-start(bf16[1024,1024]{1,0:T(8,128)(2,1)} %add_convert_fusion.1), channel_id=1, source_target_pairs={{0,1},{1,0},{2,3},{3,2},{4,5},{5,4},{6,7},{7,6},{8,9},{9,8},{10,11... | collective-permute-start | bytes 6291464 | tf_op jit(solution)/shard_map/ppermute | solution.py:468
  306.3 6.1 %copy-start.20 = (f32[1,2048]{1,0:T(1,128)S(1)}, f32[1,2048]{1,0:T(1,128)}, u32[]{:S(2)}) copy-start(f32[1,2048]{1,0:T(1,128)} %get-tuple-element.80) | copy-start | bytes 24580
  306.3 6.1 %copy-start.21 = (f32[1,2048]{1,0:T(1,128)S(1)}, f32[1,2048]{1,0:T(1,128)}, u32[]{:S(2)}) copy-start(f32[1,2048]{1,0:T(1,128)} %get-tuple-element.81) | copy-start | bytes 24580
  306.3 6.1 %copy-start.25 = (f32[1,1024]{1,0:T(1,128)S(1)}, f32[1,1024]{1,0:T(1,128)}, u32[]{:S(2)}) copy-start(f32[1,1024]{1,0:T(1,128)} %get-tuple-element.76) | copy-start | bytes 12292
  306.3 6.1 %copy-start.27 = (f32[1,1024]{1,0:T(1,128)S(1)}, f32[1,1024]{1,0:T(1,128)}, u32[]{:S(2)}) copy-start(f32[1,1024]{1,0:T(1,128)} %get-tuple-element.77) | copy-start | bytes 12292
  306.3 6.1 %copy-start.24 = (f32[1,1024]{1,0:T(1,128)S(1)}, f32[1,1024]{1,0:T(1,128)}, u32[]{:S(2)}) copy-start(f32[1,1024]{1,0:T(1,128)} %get-tuple-element.78) | copy-start | bytes 12292
  306.4 6.1 %copy-start.26 = (f32[1,1024]{1,0:T(1,128)S(1)}, f32[1,1024]{1,0:T(1,128)}, u32[]{:S(2)}) copy-start(f32[1,1024]{1,0:T(1,128)} %get-tuple-element.79) | copy-start | bytes 12292
  312.4 2.4 copy-start.9
  314.8 64.1 %copy-start.8 = (bf16[1024,1024]{1,0:T(8,128)(2,1)S(1)}, bf16[1024,1024]{1,0:T(8,128)(2,1)}, u32[]{:S(2)}) copy-start(bf16[1024,1024]{1,0:T(8,128)(2,1)} %refs_0_.1) | copy-start | bytes 6291460
  314.8 64.1 %copy-start.14 = (bf16[1024,1024]{1,0:T(8,128)(2,1)S(1)}, bf16[1024,1024]{1,0:T(8,128)(2,1)}, u32[]{:S(2)}) copy-start(bf16[1024,1024]{1,0:T(8,128)(2,1)} %get-tuple-element.64) | copy-start | bytes 6291460
  314.8 64.1 %copy-start.15 = (bf16[1024,1024]{1,0:T(8,128)(2,1)S(1)}, bf16[1024,1024]{1,0:T(8,128)(2,1)}, u32[]{:S(2)}) copy-start(bf16[1024,1024]{1,0:T(8,128)(2,1)} %get-tuple-element.74) | copy-start | bytes 6291460
  314.8 64.1 %copy-start.23 = (f32[1024]{0:T(1024)S(1)}, f32[1024]{0:T(1024)}, u32[]{:S(2)}) copy-start(f32[1024]{0:T(1024)} %param.26) | copy-start | bytes 12292
  378.9 7.4 %copy-start.19 = (f32[1024]{0:T(1024)S(1)}, f32[1024]{0:T(1024)}, u32[]{:S(2)}) copy-start(f32[1024]{0:T(1024)} %get-tuple-element.95) | copy-start | bytes 12292
  386.4 5.2 collective-permute-start.4
  542.9 5.6 copy-start.18
  542.9 7.2 %copy-start.12 = (bf16[1024,2048]{1,0:T(8,128)(2,1)S(1)}, bf16[1024,2048]{1,0:T(8,128)(2,1)}, u32[]{:S(2)}) copy-start(bf16[1024,2048]{1,0:T(8,128)(2,1)} %get-tuple-element.93) | copy-start | bytes 12582916
  550.1 4.5 copy-start.11
  (3 other events, 3.9 us)
Sparse Core Ops, SparseCore 0:
  290.3 252.5 all-reduce.2

commit v2 on v1

--- a/solution.py
+++ b/solution.py
@@ -26,6 +26,10 @@
     return lax.dot_general(a, b, (dims, ((), ())), preferred_element_type=F32)
 
 
+def cost(micros):
+    return pl.CostEstimate(flops=int(micros * 1.1e9), bytes_accessed=0, transcendentals=0)
+
+
 def norm_stats(v):
     average = jnp.mean(v, axis=-1, keepdims=True)
     centred = v - average
@@ -39,14 +43,14 @@
     return jnp.concatenate([u * cosine - w * sine, w * cosine + u * sine, x[ROT:]], axis=0)
 
 
-def project_body(place_ref, tok_ref, g_ref, gain_ref, shift_ref, w_ref, b_ref, wo_ref, cos_ref, sin_ref, *rest):
-    q_out, kt_out, vt_out, k_out, v_out, n_out, do_out = rest[-7:]
+def project_body(place_ref, tok_ref, gain_ref, shift_ref, w_ref, b_ref, cos_ref, sin_ref, *rest):
+    q_out, kt_out, vt_out, k_out, v_out, n_out = rest[-6:]
     x = tok_ref[...].astype(F32)
     centred, rstd = norm_stats(x)
     normed = (centred * rstd * gain_ref[...] + shift_ref[...]).astype(BF16)
     n_out[...] = normed
     cosine, sine = cos_ref[...], sin_ref[...]
-    width = wo_ref.shape[0]
+    width = k_out.shape[1]
 
     def head_rows(c, scale):
         p = dot(w_ref[c * width : (c + 1) * width, :], normed, NT) + b_ref[c * width : (c + 1) * width, :]
@@ -62,12 +66,11 @@
     v = head_rows(2, 1.0)
     vt_out[...] = v
     v_out[...] = v.T
-    do_out[...] = dot(wo_ref[...], g_ref[...], NT).astype(BF16)
-
-
-def project(place, tok, g, gain, shift, w_t, b_col, w_out, cosine, sine, row_len, before):
+
+
+def project(place, tok, gain, shift, w_t, b_col, cosine, sine, row_len, before):
     half, d = tok.shape
-    width = w_out.shape[0]
+    width = w_t.shape[0] // 3
     rows = 256
     steps = half // rows
     here = lambda i, place: (i, 0)
@@ -76,16 +79,14 @@
     fixed = lambda i, place: (0, 0)
     specs = [
         pl.BlockSpec((rows, d), here),
-        pl.BlockSpec((rows, d), here),
         pl.BlockSpec((1, d), fixed),
         pl.BlockSpec((1, d), fixed),
         pl.BlockSpec((3 * width, d), fixed),
         pl.BlockSpec((3 * width, 1), fixed),
-        pl.BlockSpec((width, d), fixed),
         pl.BlockSpec((ROT // 2, rows), lanes),
         pl.BlockSpec((ROT // 2, rows), lanes),
     ]
-    args = [place, tok, g, gain, shift, w_t, b_col, w_out, cosine, sine]
+    args = [place, tok, gain, shift, w_t, b_col, cosine, sine]
     aliases = {}
     if before is not None:
         specs += [pl.BlockSpec(memory_space=pl.ANY)] * 6
@@ -101,13 +102,12 @@
             in_specs=specs,
             out_specs=[pl.BlockSpec((width, rows), lanes)] * 3
             + [pl.BlockSpec((rows, width), seq)] * 2
-            + [pl.BlockSpec((rows, d), seq)]
-            + [pl.BlockSpec((width, rows), lambda i, place: (0, i))],
+            + [pl.BlockSpec((rows, d), seq)],
         ),
-        out_shape=[wide, wide, wide, tall, tall, jax.ShapeDtypeStruct((row_len, d), BF16), jax.ShapeDtypeStruct((width, half), BF16)],
+        out_shape=[wide, wide, wide, tall, tall, jax.ShapeDtypeStruct((row_len, d), BF16)],
         input_output_aliases=aliases,
-        compiler_params=pltpu.CompilerParams(vmem_limit_bytes=40 * MIB),
-        cost_estimate=pl.CostEstimate(flops=8 * half * d * width, bytes_accessed=16 * MIB, transcendentals=0),
+        compiler_params=pltpu.CompilerParams(vmem_limit_bytes=60 * MIB),
+        cost_estimate=cost(9),
         name="project",
     )(*args)
 
@@ -121,12 +121,16 @@
     return v * below, below + v * (bell * 0.3989422804014327)
 
 
-def mlp_body(*refs, first, rows):
+def mlp_body(*refs, first, again, rows, skip):
     tok_ref, g_ref, gain_ref, shift_ref, w1_ref, b1_ref, w2_ref = refs[:7]
     refs = refs[7:]
     if not first:
         dw1_in, dw2_in = refs[:2]
         refs = refs[2:]
+    if again:
+        out_in, e_in = refs[:2]
+        refs = refs[2:]
+    refs = refs[skip:]
     out_ref, e_ref, dw1_ref, dw2_ref, db1_ref, dgain_ref, dshift_ref = refs[:7]
     normed, normed_t, out_acc, back_acc, act_t, pre_t = refs[7:]
     step = pl.program_id(0)
@@ -197,33 +201,42 @@
             back = back_acc[at, :]
             dgain_ref[...] += jnp.sum(back * (centred * rstd), axis=0, keepdims=True)
             dshift_ref[...] += jnp.sum(back, axis=0, keepdims=True)
-            e_ref[at, :] = (back * gain_ref[...]).astype(BF16)
-            out_ref[at, :] = out_acc[at, :].astype(BF16)
+            e, out = back * gain_ref[...], out_acc[at, :]
+            if again:
+                e, out = e + e_in[at, :].astype(F32), out + out_in[at, :].astype(F32)
+            e_ref[at, :] = e.astype(BF16)
+            out_ref[at, :] = out.astype(BF16)
             return 0
 
         lax.fori_loop(0, blocks, finish, 0)
 
 
-def mlp(tok, g, gain, shift, w1, b1, w2, before):
+def mlp(tok, g, gain, shift, w1, b1, w2, chunk, rows, span, before=None, partial=None, after=()):
     half, d = tok.shape
-    hidden = w1.shape[1]
-    chunk = 512
-    rows = 256
+    base, chunks = span
+    hidden = chunks * chunk
     fixed = lambda j: (0, 0)
     cols = pl.BlockSpec((d, chunk), lambda j: (0, j))
     tall = pl.BlockSpec((chunk, d), lambda j: (j, 0))
     whole = pl.BlockSpec((half, d), fixed)
     line = pl.BlockSpec((1, d), fixed)
     bias = pl.BlockSpec((1, chunk), lambda j: (0, j))
+    cols_in = pl.BlockSpec((d, chunk), lambda j: (0, base + j))
+    tall_in = pl.BlockSpec((chunk, d), lambda j: (base + j, 0))
     args = [tok, g, gain, shift, w1, b1, w2]
-    specs = [whole, whole, line, line, cols, bias, tall]
+    specs = [whole, whole, line, line, cols_in, pl.BlockSpec((1, chunk), lambda j: (0, base + j)), tall_in]
     if before is not None:
         args += list(before)
-        specs += [cols, tall]
+        specs += [cols_in, tall_in]
+    if partial is not None:
+        args += list(partial)
+        specs += [whole, whole]
+    args += list(after)
+    specs += [pl.BlockSpec(memory_space=pl.ANY)] * len(after)
     shape = jax.ShapeDtypeStruct
     return pl.pallas_call(
-        functools.partial(mlp_body, first=before is None, rows=rows),
-        grid=(hidden // chunk,),
+        functools.partial(mlp_body, first=before is None, again=partial is not None, rows=rows, skip=len(after)),
+        grid=(chunks,),
         in_specs=specs,
         out_specs=[whole, whole, cols, tall, bias, line, line],
         out_shape=[
@@ -243,8 +256,8 @@
             pltpu.VMEM((chunk, half), BF16),
             pltpu.VMEM((half, chunk), BF16),
         ],
-        compiler_params=pltpu.CompilerParams(vmem_limit_bytes=56 * MIB),
-        cost_estimate=pl.CostEstimate(flops=12 * half * d * hidden, bytes_accessed=32 * MIB, transcendentals=0),
+        compiler_params=pltpu.CompilerParams(vmem_limit_bytes=60 * MIB),
+        cost_estimate=cost(44 * hidden / w1.shape[1]),
         name="feed_forward",
     )(*args)
 
@@ -253,11 +266,13 @@
     return op(x.reshape(x.shape[0] // 8, 8, x.shape[1]), axis=0)
 
 
-def attention_body(info_ref, q_ref, kt, vt, do_ref, k_ref, v_ref, start_ref, cosq_ref, sinq_ref, *rest, first, block):
+def attention_body(info_ref, q_ref, kt, vt, do_ref, k_ref, v_ref, start_ref, cosq_ref, sinq_ref, *rest, first, block, skip):
     if first:
+        rest = rest[skip:]
         o_ref, dq_ref, dk_ref, dv_ref, s_scr, e_scr = rest
     else:
-        cos_ref, sin_ref, dq_in, dk_in, dv_in, o_ref, grads_ref, s_scr, e_scr, dk_ref, dv_ref = rest
+        cos_ref, sin_ref, dq_in, dk_in, dv_in = rest[:5]
+        o_ref, grads_ref, s_scr, e_scr, dk_ref, dv_ref = rest[5 + skip :]
     step = pl.program_id(1)
     half = pl.num_programs(1) * block
     place = info_ref[0] * pl.num_programs(1) + step
@@ -361,20 +376,24 @@
             lax.fori_loop(0, row_len // block, finish, 0)
 
 
-def attention(info, q_t, k_t, v_t, do_t, k, v, start, cosine, sine, before):
-    width, row_len = q_t.shape
+def attention(info, group, q_t, k_t, v_t, do_t, k, v, start, cosine, sine, before, base_in=0, after=()):
+    base, pairs = group
+    width = pairs * PAIR
+    row_len = q_t.shape[1]
     half = do_t.shape[1]
     block = 512
     steps = half // block
     first = before is None
-    place = lambda p, i, info: (p, info[0] * steps + i)
+    place = lambda p, i, info: (base + p, info[0] * steps + i)
     line = lambda p, i, info: (0, info[0] * steps + i)
     here = pl.BlockSpec((PAIR, block), lambda p, i, info: (p, i))
     wide = pl.BlockSpec((PAIR, row_len), lambda p, i, info: (p, 0))
-    tall = pl.BlockSpec((row_len, PAIR), lambda p, i, info: (0, p))
+    of_row = pl.BlockSpec((PAIR, row_len), lambda p, i, info: (base + p, 0))
+    here_in = pl.BlockSpec((PAIR, block), lambda p, i, info: (base + p, i))
+    tall = pl.BlockSpec((row_len, PAIR), lambda p, i, info: (0, base + p))
     angle = pl.BlockSpec((ROT // 2, block), line)
     args = [info, q_t, k_t, v_t, do_t, k, v, start, cosine, sine]
-    specs = [pl.BlockSpec((PAIR, block), place), wide, wide, here, tall, tall, pl.BlockSpec((1, block), line), angle, angle]
+    specs = [pl.BlockSpec((PAIR, block), place), of_row, of_row, here_in, tall, tall, pl.BlockSpec((1, block), line), angle, angle]
     shape = jax.ShapeDtypeStruct
     scratch = [pltpu.VMEM((2, row_len, block), F32), pltpu.VMEM((2, row_len, block), BF16)]
     if first:
@@ -383,24 +402,84 @@
     else:
         table = pl.BlockSpec((ROT // 2, row_len), lambda p, i, info: (0, 0))
         args += [cosine, sine, *before]
-        specs += [table, table, pl.BlockSpec((PAIR, half), lambda p, i, info: (p, 0)), wide, wide]
+        wide_in = pl.BlockSpec((PAIR, row_len), lambda p, i, info: (base_in + p, 0))
+        specs += [table, table, pl.BlockSpec((PAIR, half), lambda p, i, info: (base_in + p, 0)), wide_in, wide_in]
         outs = [shape((width, half), BF16), shape((3, width, row_len), BF16)]
         out_specs = [here, pl.BlockSpec((3, PAIR, row_len), lambda p, i, info: (0, p, 0))]
         scratch += [pltpu.VMEM((PAIR, row_len), F32)] * 2
+    args += list(after)
+    specs += [pl.BlockSpec(memory_space=pl.ANY)] * len(after)
     return pl.pallas_call(
-        functools.partial(attention_body, first=first, block=block),
+        functools.partial(attention_body, first=first, block=block, skip=len(after)),
         grid_spec=pltpu.PrefetchScalarGridSpec(
             num_scalar_prefetch=1,
-            grid=(width // PAIR, steps),
+            grid=(pairs, steps),
             in_specs=specs,
             out_specs=out_specs,
             scratch_shapes=scratch,
         ),
         out_shape=outs,
-        compiler_params=pltpu.CompilerParams(vmem_limit_bytes=48 * MIB),
-        cost_estimate=pl.CostEstimate(flops=24 * half * half * width * 2, bytes_accessed=16 * MIB, transcendentals=0),
+        compiler_params=pltpu.CompilerParams(vmem_limit_bytes=60 * MIB),
+        cost_estimate=cost(11 * pairs),
         name="attention",
     )(*args)
+
+
+def exchange(x, bit):
+    return lax.ppermute(x, "dp", [(i, i ^ (1 << bit)) for i in range(lax.axis_size("dp"))])
+
+
+def orders():
+    bits = range(lax.axis_size("dp").bit_length() - 1)
+    return [0, *bits[1:]], [0, *bits[2:], 1]
+
+
+class Sum:
+    def __init__(self, x, order):
+        self.x = x
+        self.stages = [(True, bit) for bit in order] + [(False, bit) for bit in order[::-1]]
+        self.sent = None
+
+    def start(self):
+        if not self.stages:
+            return
+        halving, bit = self.stages[0]
+        mine = (lax.axis_index("dp") >> bit) & 1
+        if halving:
+            half = self.x.shape[0] // 2
+            self.sent = exchange(lax.dynamic_slice_in_dim(self.x, (1 - mine) * half, half, 0), bit)
+        else:
+            self.sent = exchange(self.x, bit)
+
+    def finish(self):
+        if self.sent is None:
+            return
+        halving, bit = self.stages.pop(0)
+        mine = (lax.axis_index("dp") >> bit) & 1
+        if halving:
+            half = self.x.shape[0] // 2
+            kept = lax.dynamic_slice_in_dim(self.x, mine * half, half, 0)
+            self.x = (kept.astype(F32) + self.sent.astype(F32)).astype(BF16)
+        else:
+            low = jnp.concatenate([self.x, self.sent], 0)
+            high = jnp.concatenate([self.sent, self.x], 0)
+            self.x = jnp.where(mine == 0, low, high)
+        self.sent = None
+
+
+def tick(*sums):
+    for s in sums:
+        s.finish()
+    arrived = tuple(s.x for s in sums)
+    for s in sums:
+        s.start()
+    return arrived
+
+
+def small_total(x):
+    for bit in orders()[0]:
+        x = x + exchange(x, bit)
+    return x
 
 
 def per_device(
@@ -423,11 +502,11 @@
     half, d = tokens.shape
     row_len = half * lax.axis_size("mp")
     width = qkv_weight.shape[2]
+    hidden = fc1_weight.shape[1]
     me = lax.axis_index("mp")
     swap = [(0, 1), (1, 0)]
+    y_first, z_first = orders()
     tok_far = lax.ppermute(tokens, "mp", swap)
-    cot_later, tok_far = lax.optimization_barrier((cotangent, tok_far))
-    cot_far = lax.ppermute(cot_later, "mp", swap)
 
     docs = lengths.shape[1]
     order = jnp.arange(docs)
@@ -443,7 +522,8 @@
     lows = (start[::block] // block).astype(jnp.int32).reshape(2, -1)
     near = jnp.concatenate([me[None].astype(jnp.int32), lows[me]])
     far = jnp.concatenate([(1 - me)[None].astype(jnp.int32), lows[1 - me]])
-
+    cot_later, tok_far = lax.optimization_barrier((cotangent, tok_far))
+    cot_far = lax.ppermute(cot_later, "mp", swap)
     inside = jnp.arange(half, dtype=jnp.int32)[:, None]
     g_near = jnp.where(inside < kept - me * half, cotangent, jnp.zeros((), BF16))
     g_far = jnp.where(inside < kept - (1 - me) * half, cot_far, jnp.zeros((), BF16))
@@ -454,60 +534,102 @@
     b_col = qkv_bias.reshape(3 * width, 1)
     b1 = fc1_bias[None]
 
-    mlp_near = mlp(tokens, g_near, gain2, shift2, fc1_weight, b1, fc2_weight, None)
-    front = (gain1, shift1, w_t, b_col, out_weight, cosine, sine, row_len)
-    *made, do_near = project(near[:1], tokens, g_near, *front, None)
-    q_t, k_t, v_t, k, v, normed1, do_far = project(far[:1], tok_far, g_far, *front, made)
-    o_near, dq_near, dk, dv = attention(near, q_t, k_t, v_t, do_near, k, v, start[None], cosine, sine, None)
-    mlp_far = mlp(tok_far, g_far, gain2, shift2, fc1_weight, b1, fc2_weight, mlp_near[2:4])
-    grad_fc1 = lax.psum(mlp_far[2], "dp")
-    grad_fc2 = lax.psum(mlp_far[3], "dp")
-    o_far, grads = attention(far, q_t, k_t, v_t, do_far, k, v, start[None], cosine, sine, (dq_near, dk, dv))
-
-    branch_far = dot(o_far, out_weight, TN) + mlp_far[0].astype(F32)
-    arrived = lax.ppermute(branch_far.astype(BF16), "mp", swap)
-    branch = dot(o_near, out_weight, TN) + mlp_near[0].astype(F32)
-    output = (tokens.astype(F32) + (branch + arrived.astype(F32)) + out_bias).astype(BF16)
-
-    grads = grads.reshape(3 * width, row_len)
-    grad_qkv = dot(grads, normed1).astype(BF16)
-    grad_out_w = (dot(o_near, g_near) + dot(o_far, g_far)).astype(BF16)
-    grad_qkv = lax.psum(grad_qkv, "dp")
-    grad_out_w = lax.psum(grad_out_w, "dp")
-    grad_qkv_b = jnp.sum(grads.astype(F32), axis=1)
-
-    def norm_back(place, tok, e2):
-        part = lax.dynamic_slice_in_dim(grads, place * half, half, 1)
-        back = dot(part, w_t, TN)
-        centred, rstd = norm_stats(tok.astype(F32))
+    feed = (gain2, shift2, fc1_weight, b1, fc2_weight)
+    wide = hidden // 2
+    mlp_near = mlp(tokens, g_near, *feed, wide, 256, (0, 2))
+    front = (gain1, shift1, w_t, b_col, cosine, sine, row_len)
+    made = project(near[:1], tokens, *front, None)
+    q_t, k_t, v_t, k, v, normed1 = project(far[:1], tok_far, *front, made)
+    do_near = dot(out_weight, g_near, NT).astype(BF16)
+    do_far = dot(out_weight, g_far, NT).astype(BF16)
+
+    def attend(which, group, before, base_in, do_t, after=()):
+        return attention(which, group, q_t, k_t, v_t, do_t, k, v, start[None], cosine, sine, before, base_in, after)
+
+    def branch(o, part):
+        return dot(o, out_weight, TN) + part.astype(F32)
+
+    every = (0, width // PAIR)
+    o_near, *kept_near = attend(near, every, None, 0, do_near)
+    mlp_far = mlp(tok_far, g_far, *feed, wide, 256, (0, 2), mlp_near[2:4], None, (o_near,))
+    out_far, e2_far = mlp_far[:2]
+    grad_fc1, grad_fc2 = lax.psum(mlp_far[2:4], "dp")
+
+    def rest(g_near, g_far, tok_near, tok_far, normed1, w_t, o_near, kept_near, out_near, out_far, e2_near, e2_far, do_far, early, fc1_b):
+        o_far, grads = attend(far, every, kept_near, 0, do_far)
+        grads = grads.reshape(3 * width, row_len)
+        qkv = dot(grads, normed1).astype(BF16)
+        out = (dot(o_near, g_near) + dot(o_far, g_far)).astype(BF16)
+        arrived = lax.ppermute(branch(o_far, out_far).astype(BF16), "mp", swap)
+
+        def norm_back(place, tok, e2):
+            part = lax.dynamic_slice_in_dim(grads, place * half, half, 1)
+            back = dot(part, w_t, TN)
+            centred, rstd = norm_stats(tok.astype(F32))
+            xhat = centred * rstd
+            return gain1 * back + e2.astype(F32), jnp.sum(back * xhat, axis=0), jnp.sum(back, axis=0)
+
+        e_far, dgain_far, dshift_far = norm_back(1 - me, tok_far, e2_far)
+        e_arrived = lax.ppermute(e_far.astype(BF16), "mp", swap)
+        e_near, dgain_near, dshift_near = norm_back(me, tok_near, e2_near)
+        late = jnp.stack([dgain_near + dgain_far, dshift_near + dshift_far])
+        small = jnp.concatenate([late.reshape(-1), early.reshape(-1), jnp.sum(grads.astype(F32), axis=1), fc1_b])
+        small = small_total(small.reshape(-1, 128)).reshape(-1)
+        both = small[: 5 * d].reshape(5, d)
+
+        cut = width
+        parts = [(out, y_first), (qkv[:cut], z_first), (qkv[cut : 2 * cut], y_first), (qkv[2 * cut :], y_first)]
+        parts = [Sum(x, order) for x, order in parts]
+        while any(p.stages for p in parts):
+            tick(*parts)
+
+        inputs = tok_near.astype(F32)
+        output = (inputs + (branch(o_near, out_near) + arrived.astype(F32)) + out_bias).astype(BF16)
+        e = e_near + e_arrived.astype(F32)
+        centred, rstd = norm_stats(inputs)
         xhat = centred * rstd
-        return gain1 * back + e2.astype(F32), jnp.sum(back * xhat, axis=0), jnp.sum(back, axis=0)
-
-    e_far, dgain_far, dshift_far = norm_back(1 - me, tok_far, mlp_far[1])
-    e_arrived = lax.ppermute(e_far.astype(BF16), "mp", swap)
-    e_near, dgain_near, dshift_near = norm_back(me, tokens, mlp_near[1])
-    e = e_near + e_arrived.astype(F32)
-    centred, rstd = norm_stats(tokens.astype(F32))
-    xhat = centred * rstd
-    grad_in = rstd * (e - jnp.mean(e, axis=-1, keepdims=True) - xhat * jnp.mean(e * xhat, axis=-1, keepdims=True))
-    g_wide = g_near.astype(F32)
-    grad_tokens = g_wide + grad_in
-
-    both = jnp.stack(
-        [
-            dgain_near + dgain_far,
-            dshift_near + dshift_far,
-            (mlp_near[5] + mlp_far[5])[0],
-            (mlp_near[6] + mlp_far[6])[0],
-            jnp.sum(g_wide, axis=0),
-        ]
+        grad_in = rstd * (e - jnp.mean(e, axis=-1, keepdims=True) - xhat * jnp.mean(e * xhat, axis=-1, keepdims=True))
+        grad_tokens = g_near.astype(F32) + grad_in
+        both = both + lax.ppermute(both, "mp", swap)
+        grad_qkv = jnp.transpose(jnp.stack([p.x for p in parts[1:]]), (2, 0, 1)).astype(F32)
+        grad_out_w = parts[0].x.astype(F32)
+        return output, grad_tokens, both, small[5 * d :], grad_qkv, grad_out_w
+
+    def never(g_near, g_far, tok_near, *unused):
+        zeros = jnp.zeros
+        return (
+            tok_near,
+            zeros((half, d), F32),
+            zeros((5, d), F32),
+            zeros((3 * width + hidden,), F32),
+            zeros((d, 3, width), F32),
+            zeros((width, d), F32),
+        )
+
+    early = jnp.stack([(mlp_near[5] + mlp_far[5])[0], (mlp_near[6] + mlp_far[6])[0], jnp.sum(g_near.astype(F32), axis=0)])
+    fc1_b = (mlp_near[4] + mlp_far[4])[0]
+    output, grad_tokens, both, small, grad_qkv, grad_out_w = lax.cond(
+        jnp.min(lengths) > 0,
+        rest,
+        never,
+        g_near,
+        g_far,
+        tokens,
+        tok_far,
+        normed1,
+        w_t,
+        o_near,
+        kept_near,
+        mlp_near[0],
+        out_far,
+        mlp_near[1],
+        e2_far,
+        do_far,
+        early,
+        fc1_b,
     )
-    both = both + lax.ppermute(both, "mp", swap)
-    small = jnp.concatenate([both.reshape(-1), grad_qkv_b, (mlp_near[4] + mlp_far[4])[0]])
-    small = lax.psum(small, "dp")
-    both = small[: 5 * d].reshape(5, d)
-    grad_qkv_b = small[5 * d : 5 * d + 3 * width].reshape(3, width)
-    grad_fc1_b = small[5 * d + 3 * width :]
+    grad_qkv_b = small[: 3 * width].reshape(3, width)
+    grad_fc1_b = small[3 * width :]
     return (
         output,
         grad_tokens,
@@ -515,9 +637,9 @@
         both[1],
         both[2],
         both[3],
-        jnp.transpose(grad_qkv.reshape(3, width, d), (2, 0, 1)).astype(F32),
+        grad_qkv,
         grad_qkv_b,
-        grad_out_w.astype(F32),
+        grad_out_w,
         both[4],
         grad_fc1.astype(F32),
         grad_fc1_b,

time: 575 us -> 475 us (0.83)
  waiting for transfers between devices: 164 us -> 63.9 us
  blocking collectives: 75.6 us -> 0 us
  starting transfers between devices: 5.31 us -> 48.5 us
  local copies, waits for them, and re-layouts: 18.1 us -> 34.1 us
  matrix products: 29.9 us -> 44.3 us
    psum x1 -> x0, blocking collectives: 75.6 us -> none  [per_device(): small = lax.psum(small, 'dp')]
    psum x1, waiting for transfers between devices: 73.8 us -> 0.02 us  [per_device(): grad_fc1, grad_fc2 = lax.psum(mlp_far[2:4], 'dp')]
    ppermute x3 -> x39, starting transfers between devices: 2.16 us -> 45.5 us  [the longest x36 44.6 us: exchange(): lax.ppermute(x, 'dp', [(i, i ^ 1 << bit) for i in range(lax.axis_size('dp...]
    ppermute x1, waiting for transfers between devices: 32.1 us -> 4.6 us  [per_device(): cot_far = lax.ppermute(cot_later, 'mp', swap)]
    pallas_call x2, Pallas kernels: 85.7 us -> 103 us  [attention(): pl.pallas_call(functools.partial(attention_body, first=first, block=block...]
    cond x0 -> x49, local copies, waits for them, and re-layouts: none -> 15 us
    dot_general x7 -> x9, matrix products: 29.9 us -> 44.3 us  [dot(): return lax.dot_general(a, b, (dims, ((), ())), preferred_element_type=F32)]
    reduce_sum x4 -> x2, other arithmetic: 19.1 us -> 4.95 us  [the longest x1 4.06 us: per_device(): jnp.sum(g_near.astype(F32), axis=0)]
  transfers between devices with their start and end apart: 6 -> 42, of which waited for: 4 -> 19; matrix products, arithmetic and copies ran while one was open for 10% -> 22% of each run, Pallas kernels for 10% -> 35%
where the time goes in v2:
time: 475 us; the launch traced here: 467 us
  Pallas kernels  211 us (44%)
  waiting for transfers between devices  63.9 us (13%)
  starting transfers between devices  48.5 us (10%)
  other arithmetic  47.3 us (10%)
  matrix products  44.3 us (9%)
  local copies, waits for them, and re-layouts  34.1 us (7%)
  between operations  16.3 us (3%)
    pallas_call x2, Pallas kernels, attention(): pl.pallas_call(functools.partial(attention_body, first=first, block=block...  103 us
    pallas_call x2, Pallas kernels, mlp(): pl.pallas_call(functools.partial(mlp_body, first=before is None, again=pa...  89.5 us
    ppermute x36, waiting for transfers between devices, exchange(): lax.ppermute(x, 'dp', [(i, i ^ 1 << bit) for i in range(lax.axis_size('dp...  48.4 us
    ppermute x36, starting transfers between devices, exchange(): lax.ppermute(x, 'dp', [(i, i ^ 1 << bit) for i in range(lax.axis_size('dp...  44.6 us
    dot_general x9, matrix products, dot(): return lax.dot_general(a, b, (dims, ((), ())), preferred_element_type=F32)  44.3 us
    pallas_call x2, Pallas kernels, project(): pl.pallas_call(project_body, grid_spec=pltpu.PrefetchScalarGridSpec(num_s...  18.7 us
    cond x49, local copies, waits for them, and re-layouts  15 us
  transfers between devices with their start and end apart: 42, of which 19 were waited for; matrix products, arithmetic and copies ran while one was open for 22% of the time, Pallas kernels for 35%

profile of v2, /device:TPU:0, one launch (start us, length us, event | category | flops | bytes accessed | tf_op | source)
XLA Modules:
  0.0 466.8 jit_solution(936030390912014487)
XLA Ops:
  14.1 4.6 copy.45
  19.8 4.1 convert_reduce_fusion.3
  23.9 43.4 %feed_forward.2 = (bf16[1024,1024]{1,0:T(8,128)(2,1)}, bf16[1024,1024]{1,0:T(8,128)(2,1)}, bf16[1024,2048]{1,0:T(8,128)(2,1)}, bf16[2048,1024]{1,0:T(8,128)(2,1)...) custom-call(bf16[1024,1024]{1,0:T(8,128)(2,1)S(1)} %copy.107.tok_ref.refs_0_, ...), custom_call_target="tpu_custom_call" | custom-call | flops 48399998976 | tf_op jit(solution)/shard_map/feed_forward/pallas_call | solution.py:237
  67.3 3.9 fusion.26.do_ref
  72.1 9.2 %project.2 = (bf16[512,2048]{1,0:T(8,128)(2,1)}, bf16[512,2048]{1,0:T(8,128)(2,1)}, bf16[512,2048]{1,0:T(8,128)(2,1)}, bf16[2048,512]{1,0:T(8,128)(2,1)}, bf16[2...) custom-call(s32[1]{0:T(128)} %bitcast.22.place_ref, bf16[1024,1024]{1,0:T(8,128)(2,1)S(1)} %copy.107.tok_ref.refs_0_, ...), custom_call_target="tpu_custom_call" | custom-call | flops 9900000256 | tf_op jit(solution)/shard_map/project/pallas_call | solution.py:97
  81.3 9.5 %project.3 = (bf16[512,2048]{1,0:T(8,128)(2,1)}, bf16[512,2048]{1,0:T(8,128)(2,1)}, bf16[512,2048]{1,0:T(8,128)(2,1)}, bf16[2048,512]{1,0:T(8,128)(2,1)}, bf16[2...) custom-call(s32[1]{0:T(128)} %bitcast.26.place_ref, ...), custom_call_target="tpu_custom_call", output_to_operand_aliasing={{0}: (8, {}), {1}: (9, {}), {2}: (10, {}), {3}: (11, {}), {... | custom-call | flops 9900000256 | tf_op jit(solution)/shard_map/project/pallas_call | solution.py:97
  90.8 33.3 %attention.3 = (bf16[512,1024]{1,0:T(8,128)(2,1)S(1)}, bf16[512,1024]{1,0:T(8,128)(2,1)}, f32[512,2048]{1,0:T(8,128)}, f32[512,2048]{1,0:T(8,128)}) custom-call(s32[3]{0:T(128)} %pad_add_fusion.info_ref, bf16[512,2048]{1,0:T(8,128)(2,1)} %get-tuple-element.174.q_ref, bf16[512,2048]{1,0:T(8,128)(2,1)} %get-tuple-element.175.kt, ...), custom_call_target="tpu_custom_call" | custom-call | flops 48399998976 | tf_op jit(solution)/shard_map/attention/pallas_call | solution.py:412
  124.1 4.6 collective-permute-done.40
  131.8 46.1 %feed_forward.3 = (bf16[1024,1024]{1,0:T(8,128)(2,1)}, bf16[1024,1024]{1,0:T(8,128)(2,1)}, bf16[1024,2048]{1,0:T(8,128)(2,1)}, bf16[2048,1024]{1,0:T(8,128)(2,1)...) custom-call(bf16[1024,1024]{1,0:T(8,128)(2,1)} %collective-permute-done.39.tok_ref.refs_0_, ...), custom_call_target="tpu_custom_call" | custom-call | flops 48399998976 | tf_op jit(solution)/shard_map/feed_forward/pallas_call | solution.py:237
  183.3 264.2 %conditional.1 = (bf16[1024,1024]{1,0:T(8,128)(2,1)S(1)}, f32[1024,1024]{1,0:T(8,128)}, f32[5,1024]{1,0:T(8,128)}, bf16[3584]{0:T(1024)(128)(2,1)S(1)}, f32[512,...) conditional(s32[]{:T(128)} %convert_element_type.230, ...), branch_computations={%region_4.5_spmd, %region_5.17_spmd} | conditional | flops 65696120832 | bytes 345422848 | solution.py:611
  184.6 69.8 %attention.2 = (bf16[512,1024]{1,0:T(8,128)(2,1)}, bf16[3,512,2048]{2,1,0:T(8,128)(2,1)}) custom-call(s32[3]{0:T(128)S(1)} %get-tuple-element.82.info_ref, bf16[512,2048]{1,0:T(8,128)(2,1)} %get-tuple-element.83.q_ref, bf16[512,2048]{1,0:T(8,128)(2,1)} %get-tuple-element.84.kt, bf16[512,2048]{1,0:T(8,128)(2,1)} %get-tuple-element.85.vt, ...), custom_call_target="tpu_custom_call" | custom-call | flops 48399998976 | tf_op jit(solution)/shard_map/cond/branch_1_fun/attention/pallas_call | solution.py:412
  254.4 10.2 %convolution_convert_fusion = bf16[1536,1024]{1,0:T(8,128)(2,1)S(1)} fusion(bf16[1536,2048]{1,0:T(8,128)(2,1)} %bitcast.77, bf16[2048,1024]{1,0:T(8,128)(2,1)} %get-tuple-element.109), kind=kOutput, calls=%fused_computation.28 | convolution fusion | flops 6444023808 | bytes 13631488 | tf_op jit(solution)/shard_map/cond/branch_1_fun/dot_general | solution.py:26
  281.5 10.0 %fusion.15 = (f32[1024]{0:T(1024)S(1)}, f32[1024]{0:T(1024)S(1)}, bf16[1024,1024]{1,0:T(8,128)(2,1)}) fusion(bf16[1024,1024]{1,0:T(8,128)(2,1)} %get-tuple-element.105, f32[1024]{0:T(1024)S(1)} %add_rsqrt_fusion, f32[1024]{0:T(1024)S(1)} %broadcast_multiply_fusion, bf16[1024,1024]{1,0:T(8,128)(2,1)} %get-tuple-element.104, f32[1024]{0:T(1024)S(1)} %bitcast.120, ...), kind=kOutput, calls=%fused_computation.22 | convolution fusion | flops 3231709184 | bytes 12603396 | tf_op jit(solution)/shard_map/cond/branch_1_fun/dot_general | solution.py:26
  306.9 4.3 collective-permute-done.16
  312.7 8.7 %collective-permute-done.24 = bf16[128,1024]{1,0:T(8,128)(2,1)S(1)} collective-permute-done((bf16[128,1024]{1,0:T(8,128)(2,1)S(1)}, bf16[128,1024]{1,0:T(8,128)(2,1)S(1)}, u32[]{:S(2)}, u32[]{:S(2)}) %collective-permute-start.24) | collective-permute-done | bytes 262176 | tf_op jit(solution)/shard_map/cond/branch_1_fun/ppermute | solution.py:429
  345.8 4.3 collective-permute-done.19
  350.1 3.2 collective-permute-done.27
  353.5 3.4 collective-permute-start.12
  357.0 5.5 %collective-permute-done.20 = bf16[64,1024]{1,0:T(8,128)(2,1)S(1)} collective-permute-done((bf16[64,1024]{1,0:T(8,128)(2,1)S(1)}, bf16[64,1024]{1,0:T(8,128)(2,1)S(1)}, u32[]{:S(2)}, u32[]{:S(2)}) %collective-permute-start.20) | collective-permute-done | bytes 131104 | tf_op jit(solution)/shard_map/cond/branch_1_fun/ppermute | solution.py:429
  362.5 3.2 collective-permute-start.21
  373.6 3.3 collective-permute-start.37
  377.1 6.1 %collective-permute-done.29 = bf16[128,1024]{1,0:T(8,128)(2,1)S(1)} collective-permute-done((bf16[128,1024]{1,0:T(8,128)(2,1)S(1)}, bf16[128,1024]{1,0:T(8,128)(2,1)S(1)}, u32[]{:S(2)}, u32[]{:S(2)}) %collective-permute-start.29) | collective-permute-done | bytes 262176 | tf_op jit(solution)/shard_map/cond/branch_1_fun/ppermute | solution.py:429
  385.0 3.7 collective-permute-done.37
  390.5 3.7 convert_bitcast_fusion
  396.4 7.8 %fusion.28 = (f32[1024]{0:T(1024)S(1)}, f32[1024]{0:T(1024)S(1)}, f32[1024]{0:T(1024)S(1)}, f32[1024]{0:T(1024)S(1)}, f32[1024,1024]{1,0:T(8,128)}) fusion(f32[1024]{0:T(1024)S(1)} %add_rsqrt_fusion.1, f32[1024]{0:T(1024)S(1)} %broadcast_multiply_fusion.3, bf16[1024,1024]{1,0:T(8,128)(2,1)S(1)} %get-tuple-element.78, ...), kind=kOutput, calls=%fused_computation.127 | convolution fusion | flops 3235901440 | bytes 16805892 | tf_op jit(solution)/shard_map/cond/branch_1_fun/dot_general | solution.py:26
  406.5 6.6 %copy.53 = f32[1024,3,512]{2,0,1:T(8,128)} copy(f32[1024,3,512]{0,2,1:T(8,128)} %convert_bitcast_fusion) | data formatting | bytes 12582912 | tf_op jit(solution)/shard_map/cond
  417.5 5.3 %fusion.10 = f32[1024,1024]{1,0:T(8,128)} fusion(bf16[1024,1024]{1,0:T(8,128)(2,1)S(1)} %get-tuple-element.78, f32[1024,1024]{1,0:T(8,128)} %get-tuple-element.355, bf16[1024,1024]{1,0:T(8,128)(2,1)} %get-tuple-element.98, f32[1024]{0:T(1024)S(1)} %get-tuple-element.367, f32[1024]{0:T(1024)S(1)} %get-tuple-element.368, f32[1024]{0:T(1024)S(1)} %add_rsqrt_fusion.1, ...), kind=kLoop, calls=%fused_computation.17 | loop fusion | flops 9437184 | bytes 12599296 | tf_op jit(solution)/shard_map/cond/branch_1_fun/add | solution.py:592
  425.7 7.7 %collective-permute-done = bf16[1024,1024]{1,0:T(8,128)(2,1)} collective-permute-done((bf16[1024,1024]{1,0:T(8,128)(2,1)}, bf16[1024,1024]{1,0:T(8,128)(2,1)}, u32[]{:S(2)}, u32[]{:S(2)}) %collective-permute-start) | collective-permute-done | bytes 2097184 | tf_op jit(solution)/shard_map/cond/branch_1_fun/ppermute | solution.py:563
  433.4 4.1 fusion.17
  438.4 3.1 collective-permute-done.6
  447.6 7.4 %convert_element_type.237 = f32[1024,2048]{1,0:T(8,128)} convert(bf16[1024,2048]{1,0:T(8,128)(2,1)} %get-tuple-element.353) | non-fusion elementwise | flops 2097152 | bytes 12582912 | tf_op jit(solution)/shard_map/convert_element_type | solution.py:644
  455.0 4.4 convert_element_type.238
  (276 shorter events, 105.2 us)
Async XLA Ops:
  7.2 440.4 %all-reduce.3.cloned.1.call-start = ((), (), s32[]{:S(2)}) async-start(), calls=%async_computation | async-start | bytes 16777216 | tf_op jit(solution)/shard_map/psum | solution.py:556
  8.8 72.4 %collective-permute-start.39 = (bf16[1024,1024]{1,0:T(8,128)(2,1)S(1)}, bf16[1024,1024]{1,0:T(8,128)(2,1)}, u32[]{:S(2)}, u32[]{:S(2)}) collective-permute-start(bf16[1024,1024]{1,0:T(8,128)(2,1)S(1)} %copy.107.tok_ref.refs_0_), channel_id=1, source_target_pairs={{0,1},{1,0},{2,3},{3,2},{4,5},{5,4},{6,7},{7,6},{8,9},{9,8},{10,11... | collective-permute-start | bytes 6291464 | tf_op jit(solution)/shard_map/ppermute | solution.py:509
  81.2 47.5 %collective-permute-start.40 = (bf16[1024,1024]{1,0:T(8,128)(2,1)}, bf16[1024,1024]{1,0:T(8,128)(2,1)}, u32[]{:S(2)}, u32[]{:S(2)}) collective-permute-start(bf16[1024,1024]{1,0:T(8,128)(2,1)} %param.18), channel_id=1, source_target_pairs={{0,1},{1,0},{2,3},{3,2},{4,5},{5,4},{6,7},{7,6},{8,9},{9,8},{10,11... | collective-permute-start | bytes 6291464 | tf_op jit(solution)/shard_map/ppermute | solution.py:526
  268.3 29.1 %collective-permute-start.15 = (bf16[256,1024]{1,0:T(8,128)(2,1)}, bf16[256,1024]{1,0:T(8,128)(2,1)}, u32[]{:S(2)}, u32[]{:S(2)}) collective-permute-start(bf16[256,1024]{1,0:T(8,128)(2,1)} %constant_dynamic-slice_fusion.11), channel_id=1, source_target_pairs={{0,2},{2,0},{4,6},{6,4},{8,10},{10,8},{12,14},{14,12},{16,18},{18,... | collective-permute-start | bytes 1572872 | tf_op jit(solution)/shard_map/cond/branch_1_fun/ppermute | solution.py:429
  270.2 28.9 %collective-permute-start.23 = (bf16[256,1024]{1,0:T(8,128)(2,1)}, bf16[256,1024]{1,0:T(8,128)(2,1)}, u32[]{:S(2)}, u32[]{:S(2)}) collective-permute-start(bf16[256,1024]{1,0:T(8,128)(2,1)} %constant_dynamic-slice_fusion.7), channel_id=1, source_target_pairs={{0,2},{2,0},{4,6},{6,4},{8,10},{10,8},{12,14},{14,12},{16,18},{18,... | collective-permute-start | bytes 1572872 | tf_op jit(solution)/shard_map/cond/branch_1_fun/ppermute | solution.py:429
  271.5 30.9 %collective-permute-start.7 = (bf16[256,1024]{1,0:T(8,128)(2,1)}, bf16[256,1024]{1,0:T(8,128)(2,1)}, u32[]{:S(2)}, u32[]{:S(2)}) collective-permute-start(bf16[256,1024]{1,0:T(8,128)(2,1)} %constant_dynamic-slice_fusion.15), channel_id=1, source_target_pairs={{0,2},{2,0},{4,6},{6,4},{8,10},{10,8},{12,14},{14,12},{16,18},{18,... | collective-permute-start | bytes 1572872 | tf_op jit(solution)/shard_map/cond/branch_1_fun/ppermute | solution.py:429
  276.5 29.0 %collective-permute-start.31 = (bf16[256,1024]{1,0:T(8,128)(2,1)}, bf16[256,1024]{1,0:T(8,128)(2,1)}, u32[]{:S(2)}, u32[]{:S(2)}) collective-permute-start(bf16[256,1024]{1,0:T(8,128)(2,1)} %constant_dynamic-slice_fusion.3), channel_id=1, source_target_pairs={{0,2},{2,0},{4,6},{6,4},{8,10},{10,8},{12,14},{14,12},{16,18},{18,... | collective-permute-start | bytes 1572872 | tf_op jit(solution)/shard_map/cond/branch_1_fun/ppermute | solution.py:429
  291.5 102.7 %collective-permute-start.1 = (bf16[1024,1024]{1,0:T(8,128)(2,1)}, bf16[1024,1024]{1,0:T(8,128)(2,1)}, u32[]{:S(2)}, u32[]{:S(2)}) collective-permute-start(bf16[1024,1024]{1,0:T(8,128)(2,1)} %get-tuple-element.358), channel_id=1, source_target_pairs={{0,1},{1,0},{2,3},{3,2},{4,5},{5,4},{6,7},{7,6},{8,9},{9,8},{10,11... | collective-permute-start | bytes 6291464 | tf_op jit(solution)/shard_map/cond/branch_1_fun/ppermute | solution.py:573
  299.0 12.2 %collective-permute-start.16 = (bf16[128,1024]{1,0:T(8,128)(2,1)S(1)}, bf16[128,1024]{1,0:T(8,128)(2,1)S(1)}, u32[]{:S(2)}, u32[]{:S(2)}) collective-permute-start(bf16[128,1024]{1,0:T(8,128)(2,1)S(1)} %constant_dynamic-slice_fusion.10), channel_id=1, source_target_pairs={{0,4},{2,6},{4,0},{6,2},{8,12},{10,14},{12,8},{14,10},{16,20},{18,... | collective-permute-start | bytes 786440 | tf_op jit(solution)/shard_map/cond/branch_1_fun/ppermute | solution.py:429
  300.4 21.0 %collective-permute-start.24 = (bf16[128,1024]{1,0:T(8,128)(2,1)S(1)}, bf16[128,1024]{1,0:T(8,128)(2,1)S(1)}, u32[]{:S(2)}, u32[]{:S(2)}) collective-permute-start(bf16[128,1024]{1,0:T(8,128)(2,1)S(1)} %constant_dynamic-slice_fusion.6), channel_id=1, source_target_pairs={{0,4},{2,6},{4,0},{6,2},{8,12},{10,14},{12,8},{14,10},{16,20},{18,... | collective-permute-start | bytes 786440 | tf_op jit(solution)/shard_map/cond/branch_1_fun/ppermute | solution.py:429
  304.0 19.0 %collective-permute-start.8 = (bf16[128,1024]{1,0:T(8,128)(2,1)S(1)}, bf16[128,1024]{1,0:T(8,128)(2,1)S(1)}, u32[]{:S(2)}, u32[]{:S(2)}) collective-permute-start(bf16[128,1024]{1,0:T(8,128)(2,1)S(1)} %constant_dynamic-slice_fusion.14), channel_id=1, source_target_pairs={{0,8},{2,10},{4,12},{6,14},{8,0},{10,2},{12,4},{14,6},{16,24},{18,... | collective-permute-start | bytes 786440 | tf_op jit(solution)/shard_map/cond/branch_1_fun/ppermute | solution.py:429
  306.7 19.2 %collective-permute-start.32 = (bf16[128,1024]{1,0:T(8,128)(2,1)S(1)}, bf16[128,1024]{1,0:T(8,128)(2,1)S(1)}, u32[]{:S(2)}, u32[]{:S(2)}) collective-permute-start(bf16[128,1024]{1,0:T(8,128)(2,1)S(1)} %constant_dynamic-slice_fusion.2), channel_id=1, source_target_pairs={{0,4},{2,6},{4,0},{6,2},{8,12},{10,14},{12,8},{14,10},{16,20},{18,... | collective-permute-start | bytes 786440 | tf_op jit(solution)/shard_map/cond/branch_1_fun/ppermute | solution.py:429
  311.3 16.4 %collective-permute-start.17 = (bf16[64,1024]{1,0:T(8,128)(2,1)S(1)}, bf16[64,1024]{1,0:T(8,128)(2,1)S(1)}, u32[]{:S(2)}, u32[]{:S(2)}) collective-permute-start(bf16[64,1024]{1,0:T(8,128)(2,1)S(1)} %constant_dynamic-slice_fusion.9), channel_id=1, source_target_pairs={{0,8},{2,10},{4,12},{6,14},{8,0},{10,2},{12,4},{14,6},{16,24},{18,... | collective-permute-start | bytes 393224 | tf_op jit(solution)/shard_map/cond/branch_1_fun/ppermute | solution.py:429
  321.5 10.1 %collective-permute-start.25 = (bf16[64,1024]{1,0:T(8,128)(2,1)S(1)}, bf16[64,1024]{1,0:T(8,128)(2,1)S(1)}, u32[]{:S(2)}, u32[]{:S(2)}) collective-permute-start(bf16[64,1024]{1,0:T(8,128)(2,1)S(1)} %constant_dynamic-slice_fusion.5), channel_id=1, source_target_pairs={{0,8},{2,10},{4,12},{6,14},{8,0},{10,2},{12,4},{14,6},{16,24},{18,... | collective-permute-start | bytes 393224 | tf_op jit(solution)/shard_map/cond/branch_1_fun/ppermute | solution.py:429
  323.1 10.8 %collective-permute-start.9 = (bf16[64,1024]{1,0:T(8,128)(2,1)S(1)}, bf16[64,1024]{1,0:T(8,128)(2,1)S(1)}, u32[]{:S(2)}, u32[]{:S(2)}) collective-permute-start(bf16[64,1024]{1,0:T(8,128)(2,1)S(1)} %constant_dynamic-slice_fusion.13), channel_id=1, source_target_pairs={{0,16},{2,18},{4,20},{6,22},{8,24},{10,26},{12,28},{14,30},{16,0},... | collective-permute-start | bytes 393224 | tf_op jit(solution)/shard_map/cond/branch_1_fun/ppermute | solution.py:429
  327.8 9.9 %collective-permute-start.18 = (bf16[32,1024]{1,0:T(8,128)(2,1)S(1)}, bf16[32,1024]{1,0:T(8,128)(2,1)S(1)}, u32[]{:S(2)}, u32[]{:S(2)}) collective-permute-start(bf16[32,1024]{1,0:T(8,128)(2,1)S(1)} %constant_dynamic-slice_fusion.8), channel_id=1, source_target_pairs={{0,16},{2,18},{4,20},{6,22},{8,24},{10,26},{12,28},{14,30},{16,0},... | collective-permute-start | bytes 196616 | tf_op jit(solution)/shard_map/cond/branch_1_fun/ppermute | solution.py:429
  337.7 12.3 %collective-permute-start.19 = (bf16[32,1024]{1,0:T(8,128)(2,1)S(1)}, bf16[32,1024]{1,0:T(8,128)(2,1)S(1)}, u32[]{:S(2)}, u32[]{:S(2)}) collective-permute-start(bf16[32,1024]{1,0:T(8,128)(2,1)S(1)} %add_convert_fusion.17), channel_id=1, source_target_pairs={{0,16},{2,18},{4,20},{6,22},{8,24},{10,26},{12,28},{14,30},{16,0},... | collective-permute-start | bytes 196616 | tf_op jit(solution)/shard_map/cond/branch_1_fun/ppermute | solution.py:429
  339.7 13.6 %collective-permute-start.27 = (bf16[32,1024]{1,0:T(8,128)(2,1)S(1)}, bf16[32,1024]{1,0:T(8,128)(2,1)S(1)}, u32[]{:S(2)}, u32[]{:S(2)}) collective-permute-start(bf16[32,1024]{1,0:T(8,128)(2,1)S(1)} %add_convert_fusion.16), channel_id=1, source_target_pairs={{0,16},{2,18},{4,20},{6,22},{8,24},{10,26},{12,28},{14,30},{16,0},... | collective-permute-start | bytes 196616 | tf_op jit(solution)/shard_map/cond/branch_1_fun/ppermute | solution.py:429
  340.8 12.6 %collective-permute-start.11 = (bf16[32,1024]{1,0:T(8,128)(2,1)S(1)}, bf16[32,1024]{1,0:T(8,128)(2,1)S(1)}, u32[]{:S(2)}, u32[]{:S(2)}) collective-permute-start(bf16[32,1024]{1,0:T(8,128)(2,1)S(1)} %add_convert_fusion.18), channel_id=1, source_target_pairs={{0,4},{2,6},{4,0},{6,2},{8,12},{10,14},{12,8},{14,10},{16,20},{18,... | collective-permute-start | bytes 196616 | tf_op jit(solution)/shard_map/cond/branch_1_fun/ppermute | solution.py:429
  344.7 12.2 %collective-permute-start.35 = (bf16[32,1024]{1,0:T(8,128)(2,1)S(1)}, bf16[32,1024]{1,0:T(8,128)(2,1)S(1)}, u32[]{:S(2)}, u32[]{:S(2)}) collective-permute-start(bf16[32,1024]{1,0:T(8,128)(2,1)S(1)} %add_convert_fusion.15), channel_id=1, source_target_pairs={{0,16},{2,18},{4,20},{6,22},{8,24},{10,26},{12,28},{14,30},{16,0},... | collective-permute-start | bytes 196616 | tf_op jit(solution)/shard_map/cond/branch_1_fun/ppermute | solution.py:429
  350.0 12.4 %collective-permute-start.20 = (bf16[64,1024]{1,0:T(8,128)(2,1)S(1)}, bf16[64,1024]{1,0:T(8,128)(2,1)S(1)}, u32[]{:S(2)}, u32[]{:S(2)}) collective-permute-start(bf16[64,1024]{1,0:T(8,128)(2,1)S(1)} %maximum_select_fusion.14), channel_id=1, source_target_pairs={{0,8},{2,10},{4,12},{6,14},{8,0},{10,2},{12,4},{14,6},{16,24},{18,... | collective-permute-start | bytes 393224 | tf_op jit(solution)/shard_map/cond/branch_1_fun/ppermute | solution.py:429
  353.4 14.7 %collective-permute-start.28 = (bf16[64,1024]{1,0:T(8,128)(2,1)S(1)}, bf16[64,1024]{1,0:T(8,128)(2,1)S(1)}, u32[]{:S(2)}, u32[]{:S(2)}) collective-permute-start(bf16[64,1024]{1,0:T(8,128)(2,1)S(1)} %maximum_select_fusion.15), channel_id=1, source_target_pairs={{0,8},{2,10},{4,12},{6,14},{8,0},{10,2},{12,4},{14,6},{16,24},{18,... | collective-permute-start | bytes 393224 | tf_op jit(solution)/shard_map/cond/branch_1_fun/ppermute | solution.py:429
  353.5 17.8 %collective-permute-start.12 = (bf16[64,1024]{1,0:T(8,128)(2,1)S(1)}, bf16[64,1024]{1,0:T(8,128)(2,1)S(1)}, u32[]{:S(2)}, u32[]{:S(2)}) collective-permute-start(bf16[64,1024]{1,0:T(8,128)(2,1)S(1)} %maximum_select_fusion.13), channel_id=1, source_target_pairs={{0,16},{2,18},{4,20},{6,22},{8,24},{10,26},{12,28},{14,30},{16,0},... | collective-permute-start | bytes 393224 | tf_op jit(solution)/shard_map/cond/branch_1_fun/ppermute | solution.py:429
  356.9 16.7 %collective-permute-start.36 = (bf16[64,1024]{1,0:T(8,128)(2,1)S(1)}, bf16[64,1024]{1,0:T(8,128)(2,1)S(1)}, u32[]{:S(2)}, u32[]{:S(2)}) collective-permute-start(bf16[64,1024]{1,0:T(8,128)(2,1)S(1)} %maximum_select_fusion.12), channel_id=1, source_target_pairs={{0,8},{2,10},{4,12},{6,14},{8,0},{10,2},{12,4},{14,6},{16,24},{18,... | collective-permute-start | bytes 393224 | tf_op jit(solution)/shard_map/cond/branch_1_fun/ppermute | solution.py:429
  362.5 14.4 %collective-permute-start.21 = (bf16[128,1024]{1,0:T(8,128)(2,1)S(1)}, bf16[128,1024]{1,0:T(8,128)(2,1)S(1)}, u32[]{:S(2)}, u32[]{:S(2)}) collective-permute-start(bf16[128,1024]{1,0:T(8,128)(2,1)S(1)} %maximum_select_fusion.10), channel_id=1, source_target_pairs={{0,4},{2,6},{4,0},{6,2},{8,12},{10,14},{12,8},{14,10},{16,20},{18,... | collective-permute-start | bytes 786440 | tf_op jit(solution)/shard_map/cond/branch_1_fun/ppermute | solution.py:429
  368.2 15.1 %collective-permute-start.29 = (bf16[128,1024]{1,0:T(8,128)(2,1)S(1)}, bf16[128,1024]{1,0:T(8,128)(2,1)S(1)}, u32[]{:S(2)}, u32[]{:S(2)}) collective-permute-start(bf16[128,1024]{1,0:T(8,128)(2,1)S(1)} %maximum_select_fusion.11), channel_id=1, source_target_pairs={{0,4},{2,6},{4,0},{6,2},{8,12},{10,14},{12,8},{14,10},{16,20},{18,... | collective-permute-start | bytes 786440 | tf_op jit(solution)/shard_map/cond/branch_1_fun/ppermute | solution.py:429
  371.3 13.5 %collective-permute-start.13 = (bf16[128,1024]{1,0:T(8,128)(2,1)S(1)}, bf16[128,1024]{1,0:T(8,128)(2,1)S(1)}, u32[]{:S(2)}, u32[]{:S(2)}) collective-permute-start(bf16[128,1024]{1,0:T(8,128)(2,1)S(1)} %maximum_select_fusion.9), channel_id=1, source_target_pairs={{0,8},{2,10},{4,12},{6,14},{8,0},{10,2},{12,4},{14,6},{16,24},{18,... | collective-permute-start | bytes 786440 | tf_op jit(solution)/shard_map/cond/branch_1_fun/ppermute | solution.py:429
  373.6 15.1 %collective-permute-start.37 = (bf16[128,1024]{1,0:T(8,128)(2,1)S(1)}, bf16[128,1024]{1,0:T(8,128)(2,1)S(1)}, u32[]{:S(2)}, u32[]{:S(2)}) collective-permute-start(bf16[128,1024]{1,0:T(8,128)(2,1)S(1)} %maximum_select_fusion.8), channel_id=1, source_target_pairs={{0,4},{2,6},{4,0},{6,2},{8,12},{10,14},{12,8},{14,10},{16,20},{18,... | collective-permute-start | bytes 786440 | tf_op jit(solution)/shard_map/cond/branch_1_fun/ppermute | solution.py:429
  377.0 11.8 %collective-permute-start.22 = (bf16[256,1024]{1,0:T(8,128)(2,1)S(1)}, bf16[256,1024]{1,0:T(8,128)(2,1)S(1)}, u32[]{:S(2)}, u32[]{:S(2)}) collective-permute-start(bf16[256,1024]{1,0:T(8,128)(2,1)S(1)} %maximum_select_fusion.6), channel_id=1, source_target_pairs={{0,2},{2,0},{4,6},{6,4},{8,10},{10,8},{12,14},{14,12},{16,18},{18,... | collective-permute-start | bytes 1572872 | tf_op jit(solution)/shard_map/cond/branch_1_fun/ppermute | solution.py:429
  388.7 44.7 %collective-permute-start = (bf16[1024,1024]{1,0:T(8,128)(2,1)}, bf16[1024,1024]{1,0:T(8,128)(2,1)}, u32[]{:S(2)}, u32[]{:S(2)}) collective-permute-start(bf16[1024,1024]{1,0:T(8,128)(2,1)} %add_convert_fusion.1), channel_id=1, source_target_pairs={{0,1},{1,0},{2,3},{3,2},{4,5},{5,4},{6,7},{7,6},{8,9},{9,8},{10,11... | collective-permute-start | bytes 6291464 | tf_op jit(solution)/shard_map/cond/branch_1_fun/ppermute | solution.py:563
  388.9 15.8 %collective-permute-start.38 = (bf16[256,1024]{1,0:T(8,128)(2,1)S(1)}, bf16[256,1024]{1,0:T(8,128)(2,1)S(1)}, u32[]{:S(2)}, u32[]{:S(2)}) collective-permute-start(bf16[256,1024]{1,0:T(8,128)(2,1)S(1)} %maximum_select_fusion.4), channel_id=1, source_target_pairs={{0,2},{2,0},{4,6},{6,4},{8,10},{10,8},{12,14},{14,12},{16,18},{18,... | collective-permute-start | bytes 1572872 | tf_op jit(solution)/shard_map/cond/branch_1_fun/ppermute | solution.py:429
  422.8 14.7 %collective-permute-start.5 = (f32[68,128]{1,0:T(8,128)S(1)}, f32[68,128]{1,0:T(8,128)S(1)}, u32[]{:S(2)}, u32[]{:S(2)}) collective-permute-start(f32[68,128]{1,0:T(8,128)S(1)} %add.191), channel_id=1, source_target_pairs={{0,16},{2,18},{4,20},{6,22},{8,24},{10,26},{12,28},{14,30},{16,0},... | collective-permute-start | bytes 104456 | tf_op jit(solution)/shard_map/cond/branch_1_fun/ppermute | solution.py:429
  (55 other events, 494.5 us)
Sparse Core Ops, SparseCore 0:
  178.2 237.0 all-reduce.2
